TPU v7x, 256 devices: a whole 4x4x8 slice. The times are simulated.
256 devices in a mesh: row: 4 (over z_hi, core), col: 16 (over z_lo, x), depth: 4 (over y).
Axes of the slice: x: 4, y: 4, z: 8 (z_hi: 2, z_lo: 4; z = z_hi * 4 + z_lo), core: 2. Of those that a mesh axis runs over, the one named last changes fastest.
Arguments:
- tokens: bfloat16 [1536, 6144], P(('depth', 'col'), 'row'), may hold values from -6 to 6
- w_in: bfloat16 [6144, 24576], P('row', 'col'), may hold values from -0.078125 to 0.078125
- w_out: bfloat16 [24576, 6144], P('col', 'row'), may hold values from -0.0390625 to 0.0390625
- grad_out: bfloat16 [1536, 6144], P(('depth', 'col'), 'row'), may hold values from -6 to 6
Outputs:
- layer_out: bfloat16 [1536, 6144], P(('depth', 'col'), 'row')
- grad_tokens: bfloat16 [1536, 6144], P(('depth', 'col'), 'row')
- grad_w_in: bfloat16 [6144, 24576], P(('row', 'depth'), 'col')
- grad_w_out: bfloat16 [24576, 6144], P(('col', 'depth'), 'row')
All inputs are finite; a program needn't handle non-finite values.
Results may differ from a plain program's by a relative error of at most 0.0049.
Values may be sent and summed in bfloat16 or wider, within the bound.
No kernel may reach another device: no remote copies, remote signals or barrier semaphores. Data moves between devices by JAX's collectives and lax.ppermute only.
A program may use at most 128 MiB of HBM per device.

v0:
```python
import jax
import jax.numpy as jnp
from jax import lax
from jax.sharding import PartitionSpec as P

coef = 0.7978845608


def gelu_pair(z):
    t = jnp.tanh(coef * (z + 0.044715 * z * z * z))
    value = 0.5 * z * (1.0 + t)
    slope = 0.5 * (1.0 + t) + 0.5 * z * (1.0 - t * t) * coef * (1.0 + 0.134145 * z * z)
    return (value, slope)


def inner_last(left, right):
    return lax.dot_general(
        left, right, (((1,), (1,)), ((), ())), preferred_element_type=jnp.float32
    )


def inner_first(left, right):
    return lax.dot_general(
        left, right, (((0,), (0,)), ((), ())), preferred_element_type=jnp.float32
    )


def local(tokens, w_in, w_out, grad_out):
    token_rows = lax.all_gather(tokens, "col", axis=0, tiled=True)
    pre_part = jnp.dot(token_rows, w_in, preferred_element_type=jnp.float32)
    pre = lax.psum_scatter(pre_part, "row", scatter_dimension=0, tiled=True)
    value, slope = gelu_pair(pre)
    act = value.astype(jnp.bfloat16)
    act_rows = lax.all_gather(act, "row", axis=0, tiled=True)
    out_part = jnp.dot(act_rows, w_out, preferred_element_type=jnp.float32)
    layer_out = lax.psum_scatter(out_part, "col", scatter_dimension=0, tiled=True).astype(
        jnp.bfloat16
    )
    cot_rows = lax.all_gather(grad_out, "col", axis=0, tiled=True)
    grad_part = inner_last(cot_rows, w_out)
    grad_act = lax.psum_scatter(grad_part, "row", scatter_dimension=0, tiled=True)
    grad_pre = (grad_act * slope).astype(jnp.bfloat16)
    grad_pre_rows = lax.all_gather(grad_pre, "row", axis=0, tiled=True)
    input_part = inner_last(grad_pre_rows, w_in)
    grad_tokens = lax.psum_scatter(input_part, "col", scatter_dimension=0, tiled=True).astype(
        jnp.bfloat16
    )
    first_part = inner_first(token_rows, grad_pre_rows)
    second_part = inner_first(act_rows, cot_rows)
    first_sum, second_sum = (
        lax.psum_scatter(first_part, "depth", scatter_dimension=0, tiled=True),
        lax.psum_scatter(second_part, "depth", scatter_dimension=0, tiled=True),
    )
    grad_w_in = first_sum.astype(jnp.bfloat16)
    grad_w_out = second_sum.astype(jnp.bfloat16)
    return (layer_out, grad_tokens, grad_w_in, grad_w_out)


def solution(mesh):
    return jax.shard_map(
        local,
        mesh=mesh,
        in_specs=(
            P(("depth", "col"), "row"),
            P("row", "col"),
            P("col", "row"),
            P(("depth", "col"), "row"),
        ),
        out_specs=(
            P(("depth", "col"), "row"),
            P(("depth", "col"), "row"),
            P(("row", "depth"), "col"),
            P(("col", "depth"), "row"),
        ),
        check_vma=False,
    )
```

profile of v0, /device:TPU:32, one launch (start us, length us, event | category | flops | bytes accessed | tf_op | source)
XLA Modules:
  0.0 728.9 jit_solution(13563912313347469556)
XLA Ops:
  7.2 0.0 all-gather.9.cloned.1.call-start
  7.2 0.7 all-gather.9.cloned.1.call-update
  7.9 0.0 all-gather.5.cloned.1.call-start
  7.9 0.7 all-gather.5.cloned.1.call-update
  8.6 0.0 reduce-scatter.11.cloned.1.call-start
  8.7 78.2 %all-gather.9.cloned.1.call-done = bf16[384,1536]{1,0:T(8,128)(2,1)} async-done(((bf16[24,1536]{1,0:T(8,128)(2,1)}), bf16[384,1536]{1,0:T(8,128)(2,1)}) %all-gather.9.cloned.1.call-update) | async-done | bytes 1179664 | tf_op jit(solution)/shard_map/all_gather | solution.py:39
  86.9 6.2 fusion.9
  93.1 0.0 reduce-scatter.11.cloned.1.call-update
  93.1 0.0 reduce-scatter.7.cloned.1.call-start
  93.2 75.2 %all-gather.5.cloned.1.call-done = bf16[384,1536]{1,0:T(8,128)(2,1)} async-done(((bf16[24,1536]{1,0:T(8,128)(2,1)}), bf16[384,1536]{1,0:T(8,128)(2,1)}) %all-gather.5.cloned.1.call-update) | async-done | bytes 1179664 | tf_op jit(solution)/shard_map/all_gather | solution.py:29
  168.4 6.1 fusion.7
  174.5 0.0 reduce-scatter.7.cloned.1.call-update
  174.5 0.0 all-gather.7.cloned.1.call-start
  174.5 61.4 %reduce-scatter.11.cloned.1.call-done = f32[96,1536]{1,0:T(8,128)} async-done(((f32[384,1536]{1,0:T(8,128)}), f32[96,1536]{1,0:T(8,128)}) %reduce-scatter.11.cloned.1.call-update) | async-done | bytes 589840 | tf_op jit(solution)/shard_map/reduce_scatter | solution.py:41
  235.9 59.6 %reduce-scatter.7.cloned.1.call-done = f32[96,1536]{1,0:T(8,128)} async-done(((f32[384,1536]{1,0:T(8,128)}), f32[96,1536]{1,0:T(8,128)}) %reduce-scatter.7.cloned.1.call-update) | async-done | bytes 589840 | tf_op jit(solution)/shard_map/reduce_scatter | solution.py:31
  295.5 2.5 fusion.6
  298.0 0.0 all-gather.7.cloned.1.call-update
  298.0 0.0 all-gather.11.cloned.1.call-start
  298.0 0.5 all-gather.11.cloned.1.call-update
  298.6 0.0 reduce-scatter.9.cloned.1.call-start
  298.6 28.3 %all-gather.7.cloned.1.call-done = bf16[384,1536]{1,0:T(8,128)(2,1)} async-done(((bf16[96,1536]{1,0:T(8,128)(2,1)}), bf16[384,1536]{1,0:T(8,128)(2,1)}) %all-gather.7.cloned.1.call-update) | async-done | bytes 1179664 | tf_op jit(solution)/shard_map/all_gather | solution.py:34
  326.9 6.1 fusion.8
  333.0 0.0 reduce-scatter.9.cloned.1.call-update
  333.1 0.0 reduce-scatter.13.cloned.1.call-start
  333.1 25.7 %all-gather.11.cloned.1.call-done = bf16[384,1536]{1,0:T(8,128)(2,1)} async-done(((bf16[96,1536]{1,0:T(8,128)(2,1)}), bf16[384,1536]{1,0:T(8,128)(2,1)}) %all-gather.11.cloned.1.call-update) | async-done | bytes 1179664 | tf_op jit(solution)/shard_map/all_gather | solution.py:43
  358.8 6.2 fusion.10
  364.9 0.0 copy-start.1
  364.9 0.0 copy-start.3
  364.9 0.0 reduce-scatter.13.cloned.1.call-update
  365.0 0.0 reduce-scatter.15.cloned.1.call-start
  365.0 1.2 copy-done.1
  366.2 0.4 copy-done.3
  366.6 5.3 convolution_bitcast_fusion
  371.8 0.0 reduce-scatter.15.cloned.1.call-update
  371.8 0.0 reduce-scatter.17.cloned.1.call-start
  371.9 1.2 copy-done
  373.1 0.4 copy-done.2
  373.4 5.1 fusion.11
  378.5 0.0 reduce-scatter.17.cloned.1.call-update
  378.5 61.9 %reduce-scatter.9.cloned.1.call-done = f32[24,1536]{1,0:T(8,128)} async-done(((f32[384,1536]{1,0:T(8,128)}), f32[24,1536]{1,0:T(8,128)}) %reduce-scatter.9.cloned.1.call-update) | async-done | bytes 147472 | tf_op jit(solution)/shard_map/reduce_scatter | solution.py:36
  440.4 1.6 convert_element_type.19
  442.0 85.8 %reduce-scatter.13.cloned.1.call-done = f32[24,1536]{1,0:T(8,128)} async-done(((f32[384,1536]{1,0:T(8,128)}), f32[24,1536]{1,0:T(8,128)}) %reduce-scatter.13.cloned.1.call-update) | async-done | bytes 147472 | tf_op jit(solution)/shard_map/reduce_scatter | solution.py:45
  527.7 1.6 convert_element_type.21
  529.3 96.1 %reduce-scatter.15.cloned.1.call-done = f32[384,1536]{0,1:T(8,128)} async-done(((f32[1536,1536]{0,1:T(8,128)}), f32[384,1536]{0,1:T(8,128)}) %reduce-scatter.15.cloned.1.call-update) | async-done | bytes 2359312 | tf_op jit(solution)/shard_map/reduce_scatter | solution.py:51
  625.4 1.8 convert_element_type.22
  627.2 1.5 copy.8
  628.7 90.6 %reduce-scatter.17.cloned.1.call-done = f32[384,1536]{1,0:T(8,128)} async-done(((f32[1536,1536]{1,0:T(8,128)}), f32[384,1536]{1,0:T(8,128)}) %reduce-scatter.17.cloned.1.call-update) | async-done | bytes 2359312 | tf_op jit(solution)/shard_map/reduce_scatter | solution.py:52
  719.2 2.8 convert_element_type.23
  (2 shorter events, 0.0 us)
Async XLA Ops:
  7.2 79.8 %all-gather.9.cloned.1.call-start = ((), (), s32[]{:S(2)}) async-start(), calls=%async_computation.10 | async-start | bytes 1253376 | tf_op jit(solution)/shard_map/all_gather | solution.py:39
  7.9 160.5 %all-gather.5.cloned.1.call-start = ((), (), s32[]{:S(2)}) async-start(), calls=%async_computation.6 | async-start | bytes 1253376 | tf_op jit(solution)/shard_map/all_gather | solution.py:29
  8.6 227.3 %reduce-scatter.11.cloned.1.call-start = ((), (), s32[]{:S(2)}) async-start(), calls=%async_computation.11 | async-start | bytes 2949120 | tf_op jit(solution)/shard_map/reduce_scatter | solution.py:41
  93.1 202.4 %reduce-scatter.7.cloned.1.call-start = ((), (), s32[]{:S(2)}) async-start(), calls=%async_computation.7 | async-start | bytes 2949120 | tf_op jit(solution)/shard_map/reduce_scatter | solution.py:31
  174.5 152.4 %all-gather.7.cloned.1.call-start = ((), (), s32[]{:S(2)}) async-start(), calls=%async_computation.8 | async-start | bytes 1474560 | tf_op jit(solution)/shard_map/all_gather | solution.py:34
  298.0 60.8 %all-gather.11.cloned.1.call-start = ((), (), s32[]{:S(2)}) async-start(), calls=%async_computation.12 | async-start | bytes 1474560 | tf_op jit(solution)/shard_map/all_gather | solution.py:43
  298.6 141.8 %reduce-scatter.9.cloned.1.call-start = ((), (), s32[]{:S(2)}) async-start(), calls=%async_computation.9 | async-start | bytes 2506752 | tf_op jit(solution)/shard_map/reduce_scatter | solution.py:36
  333.1 194.7 %reduce-scatter.13.cloned.1.call-start = ((), (), s32[]{:S(2)}) async-start(), calls=%async_computation.13 | async-start | bytes 2506752 | tf_op jit(solution)/shard_map/reduce_scatter | solution.py:45
  364.9 1.3 copy-start.1
  364.9 1.6 copy-start.3
  365.0 260.5 %reduce-scatter.15.cloned.1.call-start = ((), (), s32[]{:S(2)}) async-start(), calls=%async_computation.14 | async-start | bytes 11796480 | tf_op jit(solution)/shard_map/reduce_scatter | solution.py:51
  371.8 1.3 copy-start
  371.8 1.6 copy-start.2
  371.8 347.4 %reduce-scatter.17.cloned.1.call-start = ((), (), s32[]{:S(2)}) async-start(), calls=%async_computation.15 | async-start | bytes 11796480 | tf_op jit(solution)/shard_map/reduce_scatter | solution.py:52
Sparse Core Ops, SparseCore 0:
  9.8 77.0 all-gather.8
  88.7 79.6 all-gather.4
  171.2 64.7 reduce-scatter.10
  238.8 56.6 reduce-scatter.6
  298.1 28.7 all-gather.6
  329.2 29.5 all-gather.10
  361.3 79.0 reduce-scatter.8
  443.0 84.7 reduce-scatter.12
  530.4 95.0 reduce-scatter.14
  627.9 91.3 reduce-scatter.16
where the time goes:
time: 730 us; the launch traced here: 729 us
  waiting for transfers between devices  665 us (91%)
  matrix products  34.8 us (5%)
  between operations  14.2 us (2%)
  other arithmetic  10.2 us (1%)
    reduce_scatter x1, waiting for transfers between devices, local(): lax.psum_scatter(first_part, 'depth', scatter_dimension=0, tiled=True)  96.1 us
    reduce_scatter x1, waiting for transfers between devices, local(): lax.psum_scatter(second_part, 'depth', scatter_dimension=0, tiled=True)  90.6 us
    reduce_scatter x1, waiting for transfers between devices, local(): lax.psum_scatter(input_part, 'col', scatter_dimension=0, tiled=True)  85.8 us
    all_gather x1, waiting for transfers between devices, local(): cot_rows = lax.all_gather(grad_out, 'col', axis=0, tiled=True)  78.2 us
    all_gather x1, waiting for transfers between devices, local(): token_rows = lax.all_gather(tokens, 'col', axis=0, tiled=True)  75.2 us
    reduce_scatter x1, waiting for transfers between devices, local(): lax.psum_scatter(out_part, 'col', scatter_dimension=0, tiled=True)  61.9 us
    reduce_scatter x1, waiting for transfers between devices, local(): lax.psum_scatter(grad_part, 'row', scatter_dimension=0, tiled=True)  61.4 us
    reduce_scatter x1, waiting for transfers between devices, local(): pre = lax.psum_scatter(pre_part, 'row', scatter_dimension=0, tiled=True)  59.6 us
  transfers between devices with their start and end apart: 10, of which 10 were waited for; matrix products, arithmetic and copies ran while one was open for 6% of the time, Pallas kernels for 0%

commit v1 on v0

v1 whole, which is shorter than its diff:
```python
import jax
import jax.numpy as jnp
from jax import lax
from jax.sharding import PartitionSpec as P

coef = 0.7978845608
AXES = ("row", "col", "depth")
BF = jnp.bfloat16
F32 = jnp.float32


def gelu_pair(z):
    t = jnp.tanh(coef * (z + 0.044715 * z * z * z))
    value = 0.5 * z * (1.0 + t)
    slope = 0.5 * (1.0 + t) + 0.5 * z * (1.0 - t * t) * coef * (1.0 + 0.134145 * z * z)
    return (value, slope)


def dot(left, right, dims):
    return lax.dot_general(left, right, ((dims[:1], dims[1:]), ((), ())), preferred_element_type=F32)


def send(array, hi=0, core=0, lo=0, x=0, y=0):
    pairs = []
    for z_hi in range(2):
        for c in range(2):
            for z_lo in range(4):
                for i in range(4):
                    for j in range(4):
                        here = ((z_hi * 2 + c) * 16 + z_lo * 4 + i) * 4 + j
                        there = (
                            ((z_hi + hi) % 2 * 2 + (c + core) % 2) * 16 + (z_lo + lo) % 4 * 4 + (i + x) % 4
                        ) * 4 + (j + y) % 4
                        pairs.append((here, there))
    return lax.ppermute(array, AXES, pairs)


def exchange(array, turn):
    pairs = []
    for row in range(4):
        flip = 1 if row % 2 == turn else 3
        for col in range(16):
            for y in range(4):
                pairs.append(((row * 16 + col) * 4 + y, (row * 16 + col) * 4 + (y ^ flip)))
    return lax.ppermute(array, AXES, pairs)


def after(array, *others):
    return lax.optimization_barrier((array, *others))[0]


def front(token_block, cot_block, weights):
    in_mine, in_other, out_mine, out_other = weights
    other = jnp.stack([dot(token_block, in_other, (1, 0)).astype(BF), dot(cot_block, out_other, (1, 1)).astype(BF)])
    mine = jnp.stack([dot(token_block, in_mine, (1, 0)), dot(cot_block, out_mine, (1, 1))])
    return mine + send(other, core=1).astype(F32)


def cross(total):
    payload = total.astype(BF)
    return payload, send(payload, hi=1)


def middle(total, arrived):
    both = total + arrived.astype(F32)
    value, slope = gelu_pair(both[0])
    return jnp.stack([value.astype(BF), (both[1] * slope).astype(BF)])


def back(mine, other, weights):
    in_mine, in_other, out_mine, out_other = weights
    return jnp.stack(
        [
            dot(mine[0], out_mine, (1, 0)) + dot(other[0], out_other, (1, 0)),
            dot(mine[1], in_mine, (1, 1)) + dot(other[1], in_other, (1, 1)),
        ]
    )


def local(tokens, w_in, w_out, grad_out):
    core = lax.axis_index("row") % 2
    y = lax.axis_index("depth")
    weights = lax.optimization_barrier(
        (
            lax.dynamic_slice_in_dim(w_in, core * 768, 768, axis=1),
            lax.dynamic_slice_in_dim(w_in, (1 - core) * 768, 768, axis=1),
            lax.dynamic_slice_in_dim(w_out, core * 768, 768, axis=0),
            lax.dynamic_slice_in_dim(w_out, (1 - core) * 768, 768, axis=0),
        )
    )
    first = y ^ (1 + 2 * core)
    second = y ^ (3 - 2 * core)

    own = jnp.stack([tokens, grad_out])
    block0 = jnp.concatenate([own] + [send(own, lo=-k) for k in (1, 2, 3)], axis=1)
    block1 = send(block0, x=-1)
    block3 = send(block0, x=-3)
    near = jnp.concatenate([block1, block3], axis=1)
    total0 = front(block0[0], block0[1], weights)
    payload0, arrived0 = cross(total0)
    block2 = send(after(block0, near), x=-2)
    total1 = front(near[0], near[1], weights)
    payload1, arrived1 = cross(total1)
    block2 = after(block2, payload1)
    total2 = front(block2[0], block2[1], weights)
    payload2, arrived2 = cross(total2)

    def split(rows, shift):
        def quarter(q):
            return lax.dynamic_slice_in_dim(rows, (q + shift) % 4 * 384, 384, axis=1)

        return quarter(y), quarter(second), jnp.concatenate([quarter(first), quarter(y ^ 2)], axis=1)

    def pair_rows(mine, other):
        own, second_part, out = split(jnp.concatenate([mine[0], other[0]], axis=1), 2 * core)
        low = jnp.where(core == 0, mine[1], other[1])
        high = jnp.where(core == 0, other[1], mine[1])
        grad = jnp.concatenate([low, high], axis=1)
        far = exchange(jnp.concatenate([out, grad], axis=1), 0)
        return own, second_part, grad, far

    token0 = split(jnp.concatenate([block0[0], near[0]], axis=0), 0)
    cot0 = jnp.concatenate([block0[1], near[1]], axis=0)
    far0 = exchange(after(jnp.concatenate([cot0, token0[2]], axis=1), payload1), 0)
    token1 = split(block2[0], 0)
    far1 = exchange(after(jnp.concatenate([block2[1], token1[2]], axis=1), payload2), 0)

    mine0 = middle(total0, after(arrived0, payload1))
    other0 = send(mine0, core=1)
    pair0 = pair_rows(mine0, other0)

    mine1 = middle(total1, arrived1)
    other1 = send(mine1, core=1)
    pair1 = pair_rows(after(mine1, far0), other1)
    mine2 = middle(total2, after(arrived2, other1, pair1[3]))
    other2 = send(mine2, core=1)
    pair2 = pair_rows(after(mine2, pair0[3], far1), other2)

    cot_pair = jnp.concatenate([cot0, block2[1], far0[:, :1536], far1[:, :1536]], axis=0)
    token_own = jnp.concatenate([token0[0], token1[0], far0[:, 1536:1920], far1[:, 1536:1920]], axis=0)
    token_second = jnp.concatenate([token0[1], token1[1], far0[:, 1920:], far1[:, 1920:]], axis=0)
    cot_pair, token_own, token_second = lax.optimization_barrier((cot_pair, token_own, token_second))

    pairs = (pair0, pair1, pair2)

    def joined(i, cols):
        return jnp.concatenate([p[i] for p in pairs] + [p[3][:, cols] for p in pairs], axis=0)

    act_own = joined(0, slice(0, 384))
    act_second = joined(1, slice(384, 768))
    grad_pair = joined(2, slice(768, 2304))
    act_own, act_second, grad_pair = lax.optimization_barrier((act_own, act_second, grad_pair))
    out_sent = dot(act_second, cot_pair, (0, 0)).astype(BF)
    in_sent = dot(token_second, grad_pair, (0, 0)).astype(BF)
    out_kept, in_kept = lax.optimization_barrier(
        (dot(act_own, cot_pair, (0, 0)), dot(token_own, grad_pair, (0, 0)))
    )
    grad_w_out = (out_kept + exchange(out_sent, 1).astype(F32)).astype(BF)
    grad_w_in = (in_kept + exchange(in_sent, 1).astype(F32)).astype(BF)

    result0 = back(after(mine0, mine2), other0, weights)
    result1 = back(mine1, other1, weights).astype(BF)
    result2 = back(mine2, other2, weights).astype(BF)
    got1 = send(result1[:, :96], x=1)
    got3 = send(result1[:, 96:], x=3)
    got2 = send(result2, x=2)
    total = result0 + got1.astype(F32) + got3.astype(F32) + got2.astype(F32)
    total = after(total, out_sent, in_sent)
    sums = total[:, :24]
    for k in (1, 2, 3):
        sums = sums + send(total[:, 24 * k : 24 * k + 24].astype(BF), lo=k).astype(F32)
    layer_out = sums[0].astype(BF)
    grad_tokens = sums[1].astype(BF)

    return (layer_out, grad_tokens, grad_w_in, grad_w_out)


def solution(mesh):
    return jax.shard_map(
        local,
        mesh=mesh,
        in_specs=(
            P(("depth", "col"), "row"),
            P("row", "col"),
            P("col", "row"),
            P(("depth", "col"), "row"),
        ),
        out_specs=(
            P(("depth", "col"), "row"),
            P(("depth", "col"), "row"),
            P(("row", "depth"), "col"),
            P(("col", "depth"), "row"),
        ),
        check_vma=False,
    )
```

time: 730 us -> 154 us (0.21)
  waiting for transfers between devices: 665 us -> 68.6 us
  starting transfers between devices: 0.4 us -> 45 us
  matrix products: 34.8 us -> 21.5 us
  between operations: 14.2 us -> 1.35 us
    reduce_scatter x6 -> x0, waiting for transfers between devices: 455 us -> none  [the longest x1 96.1 us: local(): lax.psum_scatter(first_part, 'depth', scatter_dimension=0, tiled=True)]
    all_gather x4 -> x0, waiting for transfers between devices: 207 us -> none  [the longest x1 78.2 us: local(): cot_rows = lax.all_gather(grad_out, 'col', axis=0, tiled=True)]
    ppermute x0 -> x28, waiting for transfers between devices: none -> 68.6 us  [the longest x7 35.3 us: exchange(): return lax.ppermute(array, AXES, pairs)]
    ppermute x0 -> x28, starting transfers between devices: none -> 45 us  [the longest x21 34.3 us: send(): return lax.ppermute(array, AXES, pairs)]
    dot_general x6 -> x28, matrix products: 34.8 us -> 21.5 us  [dot(): lax.dot_general(left, right, ((dims[:1], dims[1:]), ((), ())), preferred_...]
  transfers between devices with their start and end apart: 10 -> 28, of which waited for: 10 -> 15; matrix products, arithmetic and copies ran while one was open for 6% -> 23% of each run, Pallas kernels for 0% -> 0%
where the time goes in v1:
time: 154 us
  waiting for transfers between devices  68.6 us (45%)
  starting transfers between devices  45 us (29%)
  matrix products  21.5 us (14%)
  local copies, waits for them, and re-layouts  8.88 us (6%)
  other arithmetic  8.33 us (5%)
    ppermute x7, waiting for transfers between devices, exchange(): return lax.ppermute(array, AXES, pairs)  35.3 us
    ppermute x21, starting transfers between devices, send(): return lax.ppermute(array, AXES, pairs)  34.3 us
    ppermute x21, waiting for transfers between devices, send(): return lax.ppermute(array, AXES, pairs)  33.3 us
    dot_general x28, matrix products, dot(): lax.dot_general(left, right, ((dims[:1], dims[1:]), ((), ())), preferred_...  21.5 us
    ppermute x7, starting transfers between devices, exchange(): return lax.ppermute(array, AXES, pairs)  10.7 us
    dynamic_slice x1, local copies, waits for them, and re-layouts, local(): lax.dynamic_slice_in_dim(w_in, (1 - core) * 768, 768, axis=1)  5 us
  transfers between devices with their start and end apart: 28, of which 15 were waited for; matrix products, arithmetic and copies ran while one was open for 23% of the time, Pallas kernels for 0%

profile of v1, /device:TPU:32, one launch (start us, length us, event | category | flops | bytes accessed | tf_op | source)
XLA Modules:
  0.0 153.6 jit_solution(9550009862688323992)
XLA Ops:
  0.6 1.7 %pad_maximum_fusion.16 = bf16[2,24,1536]{2,1,0:T(8,128)(2,1)} fusion(bf16[1,24,1536]{2,1,0:T(8,128)(2,1)} %bitcast.211, bf16[1,24,1536]{2,1,0:T(8,128)(2,1)} %bitcast.213), kind=kLoop, calls=%fused_computation.214 | loop fusion | flops 73728 | bytes 294912 | tf_op jit(solution)/shard_map/stack | solution.py:94
  2.3 1.9 %collective-permute-start.2 = (bf16[2,24,1536]{2,1,0:T(8,128)(2,1)}, bf16[2,24,1536]{2,1,0:T(8,128)(2,1)S(1)}, u32[]{:S(2)}, u32[]{:S(2)}) collective-permute-start(bf16[2,24,1536]{2,1,0:T(8,128)(2,1)} %pad_maximum_fusion.16), channel_id=1, source_target_pairs={{0,16},{1,17},{2,18},{3,19},{4,20},{5,21},{6,22},{7,23},{8,24},{9,... | collective-permute-start | bytes 442376 | tf_op jit(solution)/shard_map/ppermute | solution.py:35
  4.2 2.3 %collective-permute-start.1 = (bf16[2,24,1536]{2,1,0:T(8,128)(2,1)}, bf16[2,24,1536]{2,1,0:T(8,128)(2,1)S(1)}, u32[]{:S(2)}, u32[]{:S(2)}) collective-permute-start(bf16[2,24,1536]{2,1,0:T(8,128)(2,1)} %pad_maximum_fusion.16), channel_id=1, source_target_pairs={{0,32},{1,33},{2,34},{3,35},{4,36},{5,37},{6,38},{7,39},{8,40},{9,... | collective-permute-start | bytes 442376 | tf_op jit(solution)/shard_map/ppermute | solution.py:35
  6.5 1.1 collective-permute-start
  7.6 5.0 %constant_dynamic-slice_fusion.2 = (bf16[1536,768]{1,0:T(8,128)(2,1)}, bf16[1536,768]{1,0:T(8,128)(2,1)}) fusion(bf16[1536,1536]{1,0:T(8,128)(2,1)} %param.5, s32[]{:T(128)S(6)} %select_n.141, s32[]{:T(128)S(6)} %select_n.140), kind=kLoop, calls=%fused_computation.264 | loop fusion | bytes 9437192 | tf_op jit(solution)/shard_map/dynamic_slice | solution.py:86
  12.6 1.7 %constant_dynamic-slice_fusion = (bf16[768,1536]{1,0:T(8,128)(2,1)}, bf16[768,1536]{1,0:T(8,128)(2,1)S(1)}) fusion(bf16[1536,1536]{1,0:T(8,128)(2,1)S(1)} %bitcast.210, s32[]{:T(128)S(6)} %select_n.141, s32[]{:T(128)S(6)} %select_n.140), kind=kLoop, calls=%fused_computation.262 | loop fusion | bytes 9437192 | tf_op jit(solution)/shard_map/dynamic_slice | solution.py:88
  15.1 2.0 %collective-permute-done.1 = bf16[2,24,1536]{2,1,0:T(8,128)(2,1)S(1)} collective-permute-done((bf16[2,24,1536]{2,1,0:T(8,128)(2,1)}, bf16[2,24,1536]{2,1,0:T(8,128)(2,1)S(1)}, u32[]{:S(2)}, u32[]{:S(2)}) %collective-permute-start.1) | collective-permute-done | bytes 147488 | tf_op jit(solution)/shard_map/ppermute | solution.py:35
  17.1 2.0 %collective-permute-done = bf16[2,24,1536]{2,1,0:T(8,128)(2,1)S(1)} collective-permute-done((bf16[2,24,1536]{2,1,0:T(8,128)(2,1)}, bf16[2,24,1536]{2,1,0:T(8,128)(2,1)S(1)}, u32[]{:S(2)}, u32[]{:S(2)}) %collective-permute-start) | collective-permute-done | bytes 147488 | tf_op jit(solution)/shard_map/ppermute | solution.py:35
  19.2 2.8 %collective-permute-start.5 = (bf16[2,96,1536]{2,1,0:T(8,128)(2,1)S(1)}, bf16[2,96,1536]{2,1,0:T(8,128)(2,1)S(1)}, u32[]{:S(2)}, u32[]{:S(2)}) collective-permute-start(bf16[2,96,1536]{2,1,0:T(8,128)(2,1)S(1)} %pad_maximum_fusion.3), channel_id=1, source_target_pairs={{0,12},{1,13},{2,14},{3,15},{4,0},{5,1},{6,2},{7,3},{8,4},{9,5},{1... | collective-permute-start | bytes 1769480 | tf_op jit(solution)/shard_map/ppermute | solution.py:35
  22.1 0.8 fusion.15
  25.7 6.1 %collective-permute-start.4 = (bf16[2,96,768]{2,1,0:T(8,128)(2,1)S(1)}, bf16[2,96,768]{2,1,0:T(8,128)(2,1)S(1)}, u32[]{:S(2)}, u32[]{:S(2)}) collective-permute-start(bf16[2,96,768]{2,1,0:T(8,128)(2,1)S(1)} %fusion.35), channel_id=1, source_target_pairs={{0,128},{1,129},{2,130},{3,131},{4,132},{5,133},{6,134},{7,135},{8... | collective-permute-start | bytes 884744 | tf_op jit(solution)/shard_map/ppermute | solution.py:35
  31.8 3.0 %collective-permute-done.5 = bf16[2,96,1536]{2,1,0:T(8,128)(2,1)S(1)} collective-permute-done((bf16[2,96,1536]{2,1,0:T(8,128)(2,1)S(1)}, bf16[2,96,1536]{2,1,0:T(8,128)(2,1)S(1)}, u32[]{:S(2)}, u32[]{:S(2)}) %collective-permute-start.5) | collective-permute-done | bytes 589856 | tf_op jit(solution)/shard_map/ppermute | solution.py:35
  34.8 3.4 %collective-permute-done.6 = bf16[2,96,1536]{2,1,0:T(8,128)(2,1)S(1)} collective-permute-done((bf16[2,96,1536]{2,1,0:T(8,128)(2,1)S(1)}, bf16[2,96,1536]{2,1,0:T(8,128)(2,1)S(1)}, u32[]{:S(2)}, u32[]{:S(2)}) %collective-permute-start.6) | collective-permute-done | bytes 589856 | tf_op jit(solution)/shard_map/ppermute | solution.py:35
  38.2 0.9 fusion.13
  39.8 0.9 convolution_bitcast_fusion
  41.9 1.0 collective-permute-done.7
  43.1 6.1 %collective-permute-start.11 = (bf16[2,192,768]{2,1,0:T(8,128)(2,1)S(1)}, bf16[2,192,768]{2,1,0:T(8,128)(2,1)S(1)}, u32[]{:S(2)}, u32[]{:S(2)}) collective-permute-start(bf16[2,192,768]{2,1,0:T(8,128)(2,1)S(1)} %fusion.18), channel_id=1, source_target_pairs={{0,128},{1,129},{2,130},{3,131},{4,132},{5,133},{6,134},{7,135},{8... | collective-permute-start | bytes 1769480 | tf_op jit(solution)/shard_map/ppermute | solution.py:35
  49.2 9.0 %collective-permute-done.8 = bf16[2,96,1536]{2,1,0:T(8,128)(2,1)S(1)} collective-permute-done((bf16[2,96,1536]{2,1,0:T(8,128)(2,1)S(1)}, bf16[2,96,1536]{2,1,0:T(8,128)(2,1)S(1)}, u32[]{:S(2)}, u32[]{:S(2)}) %collective-permute-start.8) | collective-permute-done | bytes 589856 | tf_op jit(solution)/shard_map/ppermute | solution.py:35
  58.8 0.8 fusion.17
  59.6 0.8 convolution_bitcast_fusion.2
  60.9 1.7 %collective-permute-start.13 = (bf16[288,2304]{1,0:T(8,128)(2,1)S(1)}, bf16[288,2304]{1,0:T(8,128)(2,1)S(1)}, u32[]{:S(2)}, u32[]{:S(2)}) collective-permute-start(bf16[288,2304]{1,0:T(8,128)(2,1)S(1)} %pad_maximum_fusion), channel_id=1, source_target_pairs={{0,1},{1,0},{2,3},{3,2},{4,5},{5,4},{6,7},{7,6},{8,9},{9,8},{10,11... | collective-permute-start | bytes 3981320 | tf_op jit(solution)/shard_map/ppermute | solution.py:45
  62.6 1.6 %collective-permute-start.15 = (bf16[2,96,768]{2,1,0:T(8,128)(2,1)S(1)}, bf16[2,96,768]{2,1,0:T(8,128)(2,1)S(1)}, u32[]{:S(2)}, u32[]{:S(2)}) collective-permute-start(bf16[2,96,768]{2,1,0:T(8,128)(2,1)S(1)} %pad_maximum_fusion.13), channel_id=1, source_target_pairs={{0,64},{1,65},{2,66},{3,67},{4,68},{5,69},{6,70},{7,71},{8,72},{9,... | collective-permute-start | bytes 884744 | tf_op jit(solution)/shard_map/ppermute | solution.py:35
  65.0 5.9 %collective-permute-start.10 = (bf16[2,96,768]{2,1,0:T(8,128)(2,1)S(1)}, bf16[2,96,768]{2,1,0:T(8,128)(2,1)S(1)}, u32[]{:S(2)}, u32[]{:S(2)}) collective-permute-start(bf16[2,96,768]{2,1,0:T(8,128)(2,1)S(1)} %fusion.34), channel_id=1, source_target_pairs={{0,128},{1,129},{2,130},{3,131},{4,132},{5,133},{6,134},{7,135},{8... | collective-permute-start | bytes 884744 | tf_op jit(solution)/shard_map/ppermute | solution.py:35
  71.7 1.9 %collective-permute-start.21 = (bf16[96,2304]{1,0:T(8,128)(2,1)S(1)}, bf16[96,2304]{1,0:T(8,128)(2,1)S(1)}, u32[]{:S(2)}, u32[]{:S(2)}) collective-permute-start(bf16[96,2304]{1,0:T(8,128)(2,1)S(1)} %pad_maximum_fusion.10), channel_id=1, source_target_pairs={{0,1},{1,0},{2,3},{3,2},{4,5},{5,4},{6,7},{7,6},{8,9},{9,8},{10,11... | collective-permute-start | bytes 1327112 | tf_op jit(solution)/shard_map/ppermute | solution.py:45
  73.6 2.1 %collective-permute-done.11 = bf16[2,192,768]{2,1,0:T(8,128)(2,1)S(1)} collective-permute-done((bf16[2,192,768]{2,1,0:T(8,128)(2,1)S(1)}, bf16[2,192,768]{2,1,0:T(8,128)(2,1)S(1)}, u32[]{:S(2)}, u32[]{:S(2)}) %collective-permute-start.11) | collective-permute-done | bytes 589856 | tf_op jit(solution)/shard_map/ppermute | solution.py:35
  77.1 1.0 fusion.36
  78.1 10.1 %collective-permute-done.21 = bf16[96,2304]{1,0:T(8,128)(2,1)S(1)} collective-permute-done((bf16[96,2304]{1,0:T(8,128)(2,1)S(1)}, bf16[96,2304]{1,0:T(8,128)(2,1)S(1)}, u32[]{:S(2)}, u32[]{:S(2)}) %collective-permute-start.21) | collective-permute-done | bytes 442400 | tf_op jit(solution)/shard_map/ppermute | solution.py:45
  88.9 0.9 fusion.4
  90.3 1.7 %collective-permute-start.16 = (bf16[2,96,1536]{2,1,0:T(8,128)(2,1)S(1)}, bf16[2,96,1536]{2,1,0:T(8,128)(2,1)S(1)}, u32[]{:S(2)}, u32[]{:S(2)}) collective-permute-start(bf16[2,96,1536]{2,1,0:T(8,128)(2,1)S(1)} %get-tuple-element.56), channel_id=1, source_target_pairs={{0,4},{1,5},{2,6},{3,7},{4,8},{5,9},{6,10},{7,11},{8,12},{9,13},{1... | collective-permute-start | bytes 1769480 | tf_op jit(solution)/shard_map/ppermute | solution.py:35
  92.5 1.9 %collective-permute-start.14 = (bf16[192,2304]{1,0:T(8,128)(2,1)S(1)}, bf16[192,2304]{1,0:T(8,128)(2,1)S(1)}, u32[]{:S(2)}, u32[]{:S(2)}) collective-permute-start(bf16[192,2304]{1,0:T(8,128)(2,1)S(1)} %pad_maximum_fusion.1), channel_id=1, source_target_pairs={{0,1},{1,0},{2,3},{3,2},{4,5},{5,4},{6,7},{7,6},{8,9},{9,8},{10,11... | collective-permute-start | bytes 2654216 | tf_op jit(solution)/shard_map/ppermute | solution.py:45
  94.8 11.1 %collective-permute-done.14 = bf16[192,2304]{1,0:T(8,128)(2,1)S(1)} collective-permute-done((bf16[192,2304]{1,0:T(8,128)(2,1)S(1)}, bf16[192,2304]{1,0:T(8,128)(2,1)S(1)}, u32[]{:S(2)}, u32[]{:S(2)}) %collective-permute-start.14) | collective-permute-done | bytes 884768 | tf_op jit(solution)/shard_map/ppermute | solution.py:45
  106.2 0.8 fusion.91
  108.8 0.8 fusion.3
  110.7 0.8 fusion.8
  112.5 1.6 %collective-permute-start.22 = (bf16[96,2304]{1,0:T(8,128)(2,1)S(1)}, bf16[96,2304]{1,0:T(8,128)(2,1)S(1)}, u32[]{:S(2)}, u32[]{:S(2)}) collective-permute-start(bf16[96,2304]{1,0:T(8,128)(2,1)S(1)} %pad_maximum_fusion.11), channel_id=1, source_target_pairs={{0,1},{1,0},{2,3},{3,2},{4,5},{5,4},{6,7},{7,6},{8,9},{9,8},{10,11... | collective-permute-start | bytes 1327112 | tf_op jit(solution)/shard_map/ppermute | solution.py:45
  114.3 6.6 %collective-permute-done.22 = bf16[96,2304]{1,0:T(8,128)(2,1)S(1)} collective-permute-done((bf16[96,2304]{1,0:T(8,128)(2,1)S(1)}, bf16[96,2304]{1,0:T(8,128)(2,1)S(1)}, u32[]{:S(2)}, u32[]{:S(2)}) %collective-permute-start.22) | collective-permute-done | bytes 442400 | tf_op jit(solution)/shard_map/ppermute | solution.py:45
  121.0 1.1 convolution_convert_fusion
  122.1 3.0 %collective-permute-start.26 = (bf16[384,1536]{1,0:T(8,128)(2,1)S(1)}, bf16[384,1536]{1,0:T(8,128)(2,1)S(1)}, u32[]{:S(2)}, u32[]{:S(2)}) collective-permute-start(bf16[384,1536]{1,0:T(8,128)(2,1)S(1)} %convolution_convert_fusion), channel_id=1, source_target_pairs={{0,3},{1,2},{2,1},{3,0},{4,7},{5,6},{6,5},{7,4},{8,11},{9,10},{10,... | collective-permute-start | bytes 3538952 | tf_op jit(solution)/shard_map/ppermute | solution.py:45
  125.1 1.1 convolution_convert_fusion.1
  126.6 1.1 fusion.142
  127.7 1.4 collective-permute-done.19
  129.7 1.1 collective-permute-start.24
  130.8 2.2 %collective-permute-start.23 = (bf16[2,24,1536]{2,1,0:T(8,128)(2,1)S(1)}, bf16[2,24,1536]{2,1,0:T(8,128)(2,1)S(1)}, u32[]{:S(2)}, u32[]{:S(2)}) collective-permute-start(bf16[2,24,1536]{2,1,0:T(8,128)(2,1)S(1)} %get-tuple-element.70), channel_id=1, source_target_pairs={{0,16},{1,17},{2,18},{3,19},{4,20},{5,21},{6,22},{7,23},{8,24},{9,... | collective-permute-start | bytes 442376 | tf_op jit(solution)/shard_map/ppermute | solution.py:35
  132.9 1.1 fusion.143
  134.0 8.4 %collective-permute-done.25 = bf16[2,24,1536]{2,1,0:T(8,128)(2,1)S(1)} collective-permute-done((bf16[2,24,1536]{2,1,0:T(8,128)(2,1)S(1)}, bf16[2,24,1536]{2,1,0:T(8,128)(2,1)S(1)}, u32[]{:S(2)}, u32[]{:S(2)}) %collective-permute-start.25) | collective-permute-done | bytes 147488 | tf_op jit(solution)/shard_map/ppermute | solution.py:35
  143.3 1.4 add_convert_fusion.1
  144.7 7.5 %collective-permute-done.27 = bf16[384,1536]{1,0:T(8,128)(2,1)S(1)} collective-permute-done((bf16[384,1536]{1,0:T(8,128)(2,1)S(1)}, bf16[384,1536]{1,0:T(8,128)(2,1)S(1)}, u32[]{:S(2)}, u32[]{:S(2)}) %collective-permute-start.27) | collective-permute-done | bytes 1179680 | tf_op jit(solution)/shard_map/ppermute | solution.py:45
  152.2 1.4 add_convert_fusion
  (121 shorter events, 17.4 us)
Async XLA Ops:
  0.6 12.0 %slice-start = ((s8[4718592]{0:T(1024)(128)(4,1)}), s8[524288]{0:T(1024)(128)(4,1)S(1)}, s32[]{:S(2)}) async-start(s8[4718592]{0:T(1024)(128)(4,1)} %bitcast.209), calls=%async_computation | async-start | bytes 1048576
  2.3 12.8 %collective-permute-start.2 = (bf16[2,24,1536]{2,1,0:T(8,128)(2,1)}, bf16[2,24,1536]{2,1,0:T(8,128)(2,1)S(1)}, u32[]{:S(2)}, u32[]{:S(2)}) collective-permute-start(bf16[2,24,1536]{2,1,0:T(8,128)(2,1)} %pad_maximum_fusion.16), channel_id=1, source_target_pairs={{0,16},{1,17},{2,18},{3,19},{4,20},{5,21},{6,22},{7,23},{8,24},{9,... | collective-permute-start | bytes 442376 | tf_op jit(solution)/shard_map/ppermute | solution.py:35
  4.2 12.9 %collective-permute-start.1 = (bf16[2,24,1536]{2,1,0:T(8,128)(2,1)}, bf16[2,24,1536]{2,1,0:T(8,128)(2,1)S(1)}, u32[]{:S(2)}, u32[]{:S(2)}) collective-permute-start(bf16[2,24,1536]{2,1,0:T(8,128)(2,1)} %pad_maximum_fusion.16), channel_id=1, source_target_pairs={{0,32},{1,33},{2,34},{3,35},{4,36},{5,37},{6,38},{7,39},{8,40},{9,... | collective-permute-start | bytes 442376 | tf_op jit(solution)/shard_map/ppermute | solution.py:35
  6.5 12.6 %collective-permute-start = (bf16[2,24,1536]{2,1,0:T(8,128)(2,1)}, bf16[2,24,1536]{2,1,0:T(8,128)(2,1)S(1)}, u32[]{:S(2)}, u32[]{:S(2)}) collective-permute-start(bf16[2,24,1536]{2,1,0:T(8,128)(2,1)} %pad_maximum_fusion.16), channel_id=1, source_target_pairs={{0,48},{1,49},{2,50},{3,51},{4,52},{5,53},{6,54},{7,55},{8,56},{9,... | collective-permute-start | bytes 442376 | tf_op jit(solution)/shard_map/ppermute | solution.py:35
  7.6 5.0 %slice-start.1 = ((s8[4718592]{0:T(1024)(128)(4,1)}), s8[4194304]{0:T(1024)(128)(4,1)S(1)}, s32[]{:S(2)}) async-start(s8[4718592]{0:T(1024)(128)(4,1)} %bitcast.209), calls=%async_computation.1 | async-start | bytes 8388608
  12.6 6.5 %copy-start.3 = (bf16[24,1536]{1,0:T(8,128)(2,1)S(1)}, bf16[24,1536]{1,0:T(8,128)(2,1)}, u32[]{:S(2)}) copy-start(bf16[24,1536]{1,0:T(8,128)(2,1)} %param.7) | copy-start | bytes 221188
  12.6 6.5 %copy-start.4 = (bf16[24,1536]{1,0:T(8,128)(2,1)S(1)}, bf16[24,1536]{1,0:T(8,128)(2,1)}, u32[]{:S(2)}) copy-start(bf16[24,1536]{1,0:T(8,128)(2,1)} %param.4) | copy-start | bytes 221188
  14.3 7.7 %copy-start.1 = (bf16[768,1536]{1,0:T(8,128)(2,1)S(1)}, bf16[768,1536]{1,0:T(8,128)(2,1)}, u32[]{:S(2)}) copy-start(bf16[768,1536]{1,0:T(8,128)(2,1)} %get-tuple-element.29) | copy-start | bytes 7077892
  19.2 3.8 %copy-start = (bf16[1536,768]{1,0:T(8,128)(2,1)S(1)}, bf16[1536,768]{1,0:T(8,128)(2,1)}, u32[]{:S(2)}) copy-start(bf16[1536,768]{1,0:T(8,128)(2,1)} %get-tuple-element.28) | copy-start | bytes 7077892
  19.2 15.6 %collective-permute-start.5 = (bf16[2,96,1536]{2,1,0:T(8,128)(2,1)S(1)}, bf16[2,96,1536]{2,1,0:T(8,128)(2,1)S(1)}, u32[]{:S(2)}, u32[]{:S(2)}) collective-permute-start(bf16[2,96,1536]{2,1,0:T(8,128)(2,1)S(1)} %pad_maximum_fusion.3), channel_id=1, source_target_pairs={{0,12},{1,13},{2,14},{3,15},{4,0},{5,1},{6,2},{7,3},{8,4},{9,5},{1... | collective-permute-start | bytes 1769480 | tf_op jit(solution)/shard_map/ppermute | solution.py:35
  22.0 16.2 %collective-permute-start.6 = (bf16[2,96,1536]{2,1,0:T(8,128)(2,1)S(1)}, bf16[2,96,1536]{2,1,0:T(8,128)(2,1)S(1)}, u32[]{:S(2)}, u32[]{:S(2)}) collective-permute-start(bf16[2,96,1536]{2,1,0:T(8,128)(2,1)S(1)} %pad_maximum_fusion.3), channel_id=1, source_target_pairs={{0,4},{1,5},{2,6},{3,7},{4,8},{5,9},{6,10},{7,11},{8,12},{9,13},{1... | collective-permute-start | bytes 1769480 | tf_op jit(solution)/shard_map/ppermute | solution.py:35
  23.5 1.7 %copy-start.2 = (bf16[1536,768]{1,0:T(8,128)(2,1)S(1)}, bf16[1536,768]{1,0:T(8,128)(2,1)}, u32[]{:S(2)}) copy-start(bf16[1536,768]{1,0:T(8,128)(2,1)} %get-tuple-element.26) | copy-start | bytes 7077892
  23.5 2.1 %collective-permute-start.3 = (bf16[2,96,768]{2,1,0:T(8,128)(2,1)S(1)}, bf16[2,96,768]{2,1,0:T(8,128)(2,1)S(1)}, u32[]{:S(2)}, u32[]{:S(2)}) collective-permute-start(bf16[2,96,768]{2,1,0:T(8,128)(2,1)S(1)} %pad_maximum_fusion.12), channel_id=1, source_target_pairs={{0,64},{1,65},{2,66},{3,67},{4,68},{5,69},{6,70},{7,71},{8,72},{9,... | collective-permute-start | bytes 884744 | tf_op jit(solution)/shard_map/ppermute | solution.py:35
  25.7 34.7 %collective-permute-start.4 = (bf16[2,96,768]{2,1,0:T(8,128)(2,1)S(1)}, bf16[2,96,768]{2,1,0:T(8,128)(2,1)S(1)}, u32[]{:S(2)}, u32[]{:S(2)}) collective-permute-start(bf16[2,96,768]{2,1,0:T(8,128)(2,1)S(1)} %fusion.35), channel_id=1, source_target_pairs={{0,128},{1,129},{2,130},{3,131},{4,132},{5,133},{6,134},{7,135},{8... | collective-permute-start | bytes 884744 | tf_op jit(solution)/shard_map/ppermute | solution.py:35
  40.8 2.1 %collective-permute-start.7 = (bf16[2,192,768]{2,1,0:T(8,128)(2,1)S(1)}, bf16[2,192,768]{2,1,0:T(8,128)(2,1)S(1)}, u32[]{:S(2)}, u32[]{:S(2)}) collective-permute-start(bf16[2,192,768]{2,1,0:T(8,128)(2,1)S(1)} %pad_maximum_fusion.4), channel_id=1, source_target_pairs={{0,64},{1,65},{2,66},{3,67},{4,68},{5,69},{6,70},{7,71},{8,72},{9,... | collective-permute-start | bytes 1769480 | tf_op jit(solution)/shard_map/ppermute | solution.py:35
  40.9 17.3 %collective-permute-start.8 = (bf16[2,96,1536]{2,1,0:T(8,128)(2,1)S(1)}, bf16[2,96,1536]{2,1,0:T(8,128)(2,1)S(1)}, u32[]{:S(2)}, u32[]{:S(2)}) collective-permute-start(bf16[2,96,1536]{2,1,0:T(8,128)(2,1)S(1)} %pad_maximum_fusion.3), channel_id=1, source_target_pairs={{0,8},{1,9},{2,10},{3,11},{4,12},{5,13},{6,14},{7,15},{8,0},{9,1},... | collective-permute-start | bytes 1769480 | tf_op jit(solution)/shard_map/ppermute | solution.py:35
  43.1 32.6 %collective-permute-start.11 = (bf16[2,192,768]{2,1,0:T(8,128)(2,1)S(1)}, bf16[2,192,768]{2,1,0:T(8,128)(2,1)S(1)}, u32[]{:S(2)}, u32[]{:S(2)}) collective-permute-start(bf16[2,192,768]{2,1,0:T(8,128)(2,1)S(1)} %fusion.18), channel_id=1, source_target_pairs={{0,128},{1,129},{2,130},{3,131},{4,132},{5,133},{6,134},{7,135},{8... | collective-permute-start | bytes 1769480 | tf_op jit(solution)/shard_map/ppermute | solution.py:35
  60.8 4.2 %collective-permute-start.9 = (bf16[2,96,768]{2,1,0:T(8,128)(2,1)S(1)}, bf16[2,96,768]{2,1,0:T(8,128)(2,1)S(1)}, u32[]{:S(2)}, u32[]{:S(2)}) collective-permute-start(bf16[2,96,768]{2,1,0:T(8,128)(2,1)S(1)} %pad_maximum_fusion.14), channel_id=1, source_target_pairs={{0,64},{1,65},{2,66},{3,67},{4,68},{5,69},{6,70},{7,71},{8,72},{9,... | collective-permute-start | bytes 884744 | tf_op jit(solution)/shard_map/ppermute | solution.py:35
  60.9 31.2 %collective-permute-start.13 = (bf16[288,2304]{1,0:T(8,128)(2,1)S(1)}, bf16[288,2304]{1,0:T(8,128)(2,1)S(1)}, u32[]{:S(2)}, u32[]{:S(2)}) collective-permute-start(bf16[288,2304]{1,0:T(8,128)(2,1)S(1)} %pad_maximum_fusion), channel_id=1, source_target_pairs={{0,1},{1,0},{2,3},{3,2},{4,5},{5,4},{6,7},{7,6},{8,9},{9,8},{10,11... | collective-permute-start | bytes 3981320 | tf_op jit(solution)/shard_map/ppermute | solution.py:45
  62.6 8.4 %collective-permute-start.15 = (bf16[2,96,768]{2,1,0:T(8,128)(2,1)S(1)}, bf16[2,96,768]{2,1,0:T(8,128)(2,1)S(1)}, u32[]{:S(2)}, u32[]{:S(2)}) collective-permute-start(bf16[2,96,768]{2,1,0:T(8,128)(2,1)S(1)} %pad_maximum_fusion.13), channel_id=1, source_target_pairs={{0,64},{1,65},{2,66},{3,67},{4,68},{5,69},{6,70},{7,71},{8,72},{9,... | collective-permute-start | bytes 884744 | tf_op jit(solution)/shard_map/ppermute | solution.py:35
  65.0 29.7 %collective-permute-start.10 = (bf16[2,96,768]{2,1,0:T(8,128)(2,1)S(1)}, bf16[2,96,768]{2,1,0:T(8,128)(2,1)S(1)}, u32[]{:S(2)}, u32[]{:S(2)}) collective-permute-start(bf16[2,96,768]{2,1,0:T(8,128)(2,1)S(1)} %fusion.34), channel_id=1, source_target_pairs={{0,128},{1,129},{2,130},{3,131},{4,132},{5,133},{6,134},{7,135},{8... | collective-permute-start | bytes 884744 | tf_op jit(solution)/shard_map/ppermute | solution.py:35
  71.4 37.4 %collective-permute-start.20 = (bf16[96,2304]{1,0:T(8,128)(2,1)S(1)}, bf16[96,2304]{1,0:T(8,128)(2,1)S(1)}, u32[]{:S(2)}, u32[]{:S(2)}) collective-permute-start(bf16[96,2304]{1,0:T(8,128)(2,1)S(1)} %pad_maximum_fusion.9), channel_id=1, source_target_pairs={{0,1},{1,0},{2,3},{3,2},{4,5},{5,4},{6,7},{7,6},{8,9},{9,8},{10,11... | collective-permute-start | bytes 1327112 | tf_op jit(solution)/shard_map/ppermute | solution.py:45
  71.7 16.6 %collective-permute-start.21 = (bf16[96,2304]{1,0:T(8,128)(2,1)S(1)}, bf16[96,2304]{1,0:T(8,128)(2,1)S(1)}, u32[]{:S(2)}, u32[]{:S(2)}) collective-permute-start(bf16[96,2304]{1,0:T(8,128)(2,1)S(1)} %pad_maximum_fusion.10), channel_id=1, source_target_pairs={{0,1},{1,0},{2,3},{3,2},{4,5},{5,4},{6,7},{7,6},{8,9},{9,8},{10,11... | collective-permute-start | bytes 1327112 | tf_op jit(solution)/shard_map/ppermute | solution.py:45
  76.3 12.0 %collective-permute-start.12 = (bf16[2,192,768]{2,1,0:T(8,128)(2,1)S(1)}, bf16[2,192,768]{2,1,0:T(8,128)(2,1)S(1)}, u32[]{:S(2)}, u32[]{:S(2)}) collective-permute-start(bf16[2,192,768]{2,1,0:T(8,128)(2,1)S(1)} %pad_maximum_fusion.5), channel_id=1, source_target_pairs={{0,64},{1,65},{2,66},{3,67},{4,68},{5,69},{6,70},{7,71},{8,72},{9,... | collective-permute-start | bytes 1769480 | tf_op jit(solution)/shard_map/ppermute | solution.py:35
  89.9 37.8 %collective-permute-start.17 = (bf16[2,96,1536]{2,1,0:T(8,128)(2,1)S(1)}, bf16[2,96,1536]{2,1,0:T(8,128)(2,1)S(1)}, u32[]{:S(2)}, u32[]{:S(2)}) collective-permute-start(bf16[2,96,1536]{2,1,0:T(8,128)(2,1)S(1)} %get-tuple-element.57), channel_id=1, source_target_pairs={{0,12},{1,13},{2,14},{3,15},{4,0},{5,1},{6,2},{7,3},{8,4},{9,5},{1... | collective-permute-start | bytes 1769480 | tf_op jit(solution)/shard_map/ppermute | solution.py:35
  90.3 37.4 %collective-permute-start.16 = (bf16[2,96,1536]{2,1,0:T(8,128)(2,1)S(1)}, bf16[2,96,1536]{2,1,0:T(8,128)(2,1)S(1)}, u32[]{:S(2)}, u32[]{:S(2)}) collective-permute-start(bf16[2,96,1536]{2,1,0:T(8,128)(2,1)S(1)} %get-tuple-element.56), channel_id=1, source_target_pairs={{0,4},{1,5},{2,6},{3,7},{4,8},{5,9},{6,10},{7,11},{8,12},{9,13},{1... | collective-permute-start | bytes 1769480 | tf_op jit(solution)/shard_map/ppermute | solution.py:35
  92.5 13.4 %collective-permute-start.14 = (bf16[192,2304]{1,0:T(8,128)(2,1)S(1)}, bf16[192,2304]{1,0:T(8,128)(2,1)S(1)}, u32[]{:S(2)}, u32[]{:S(2)}) collective-permute-start(bf16[192,2304]{1,0:T(8,128)(2,1)S(1)} %pad_maximum_fusion.1), channel_id=1, source_target_pairs={{0,1},{1,0},{2,3},{3,2},{4,5},{5,4},{6,7},{7,6},{8,9},{9,8},{10,11... | collective-permute-start | bytes 2654216 | tf_op jit(solution)/shard_map/ppermute | solution.py:45
  107.6 3.2 %collective-permute-start.18 = (bf16[2,96,768]{2,1,0:T(8,128)(2,1)S(1)}, bf16[2,96,768]{2,1,0:T(8,128)(2,1)S(1)}, u32[]{:S(2)}, u32[]{:S(2)}) collective-permute-start(bf16[2,96,768]{2,1,0:T(8,128)(2,1)S(1)} %pad_maximum_fusion.15), channel_id=1, source_target_pairs={{0,64},{1,65},{2,66},{3,67},{4,68},{5,69},{6,70},{7,71},{8,72},{9,... | collective-permute-start | bytes 884744 | tf_op jit(solution)/shard_map/ppermute | solution.py:35
  112.2 17.0 %collective-permute-start.19 = (bf16[2,96,1536]{2,1,0:T(8,128)(2,1)S(1)}, bf16[2,96,1536]{2,1,0:T(8,128)(2,1)S(1)}, u32[]{:S(2)}, u32[]{:S(2)}) collective-permute-start(bf16[2,96,1536]{2,1,0:T(8,128)(2,1)S(1)} %pad_maximum_fusion.6), channel_id=1, source_target_pairs={{0,8},{1,9},{2,10},{3,11},{4,12},{5,13},{6,14},{7,15},{8,0},{9,1},... | collective-permute-start | bytes 1769480 | tf_op jit(solution)/shard_map/ppermute | solution.py:35
  112.5 8.4 %collective-permute-start.22 = (bf16[96,2304]{1,0:T(8,128)(2,1)S(1)}, bf16[96,2304]{1,0:T(8,128)(2,1)S(1)}, u32[]{:S(2)}, u32[]{:S(2)}) collective-permute-start(bf16[96,2304]{1,0:T(8,128)(2,1)S(1)} %pad_maximum_fusion.11), channel_id=1, source_target_pairs={{0,1},{1,0},{2,3},{3,2},{4,5},{5,4},{6,7},{7,6},{8,9},{9,8},{10,11... | collective-permute-start | bytes 1327112 | tf_op jit(solution)/shard_map/ppermute | solution.py:45
  122.1 21.3 %collective-permute-start.26 = (bf16[384,1536]{1,0:T(8,128)(2,1)S(1)}, bf16[384,1536]{1,0:T(8,128)(2,1)S(1)}, u32[]{:S(2)}, u32[]{:S(2)}) collective-permute-start(bf16[384,1536]{1,0:T(8,128)(2,1)S(1)} %convolution_convert_fusion), channel_id=1, source_target_pairs={{0,3},{1,2},{2,1},{3,0},{4,7},{5,6},{6,5},{7,4},{8,11},{9,10},{10,... | collective-permute-start | bytes 3538952 | tf_op jit(solution)/shard_map/ppermute | solution.py:45
  126.2 26.0 %collective-permute-start.27 = (bf16[384,1536]{1,0:T(8,128)(2,1)S(1)}, bf16[384,1536]{1,0:T(8,128)(2,1)S(1)}, u32[]{:S(2)}, u32[]{:S(2)}) collective-permute-start(bf16[384,1536]{1,0:T(8,128)(2,1)S(1)} %convolution_convert_fusion.1), channel_id=1, source_target_pairs={{0,3},{1,2},{2,1},{3,0},{4,7},{5,6},{6,5},{7,4},{8,11},{9,10},{10,... | collective-permute-start | bytes 3538952 | tf_op jit(solution)/shard_map/ppermute | solution.py:45
  129.6 12.9 %collective-permute-start.25 = (bf16[2,24,1536]{2,1,0:T(8,128)(2,1)S(1)}, bf16[2,24,1536]{2,1,0:T(8,128)(2,1)S(1)}, u32[]{:S(2)}, u32[]{:S(2)}) collective-permute-start(bf16[2,24,1536]{2,1,0:T(8,128)(2,1)S(1)} %get-tuple-element.71), channel_id=1, source_target_pairs={{0,48},{1,49},{2,50},{3,51},{4,52},{5,53},{6,54},{7,55},{8,56},{9,... | collective-permute-start | bytes 442376 | tf_op jit(solution)/shard_map/ppermute | solution.py:35
  129.7 12.8 %collective-permute-start.24 = (bf16[2,24,1536]{2,1,0:T(8,128)(2,1)S(1)}, bf16[2,24,1536]{2,1,0:T(8,128)(2,1)S(1)}, u32[]{:S(2)}, u32[]{:S(2)}) collective-permute-start(bf16[2,24,1536]{2,1,0:T(8,128)(2,1)S(1)} %get-tuple-element.72), channel_id=1, source_target_pairs={{0,32},{1,33},{2,34},{3,35},{4,36},{5,37},{6,38},{7,39},{8,40},{9,... | collective-permute-start | bytes 442376 | tf_op jit(solution)/shard_map/ppermute | solution.py:35
  130.8 11.8 %collective-permute-start.23 = (bf16[2,24,1536]{2,1,0:T(8,128)(2,1)S(1)}, bf16[2,24,1536]{2,1,0:T(8,128)(2,1)S(1)}, u32[]{:S(2)}, u32[]{:S(2)}) collective-permute-start(bf16[2,24,1536]{2,1,0:T(8,128)(2,1)S(1)} %get-tuple-element.70), channel_id=1, source_target_pairs={{0,16},{1,17},{2,18},{3,19},{4,20},{5,21},{6,22},{7,23},{8,24},{9,... | collective-permute-start | bytes 442376 | tf_op jit(solution)/shard_map/ppermute | solution.py:35

commit v2 on v1

--- a/solution.py
+++ b/solution.py
@@ -98,7 +98,7 @@
     near = jnp.concatenate([block1, block3], axis=1)
     total0 = front(block0[0], block0[1], weights)
     payload0, arrived0 = cross(total0)
-    block2 = send(after(block0, near), x=-2)
+    block2 = jnp.stack([send(block1[0], x=-1), send(block3[1], x=1)])
     total1 = front(near[0], near[1], weights)
     payload1, arrived1 = cross(total1)
     block2 = after(block2, payload1)
@@ -116,62 +116,64 @@
         low = jnp.where(core == 0, mine[1], other[1])
         high = jnp.where(core == 0, other[1], mine[1])
         grad = jnp.concatenate([low, high], axis=1)
-        far = exchange(jnp.concatenate([out, grad], axis=1), 0)
-        return own, second_part, grad, far
+        return own, second_part, grad, jnp.concatenate([out, grad], axis=1)
 
     token0 = split(jnp.concatenate([block0[0], near[0]], axis=0), 0)
     cot0 = jnp.concatenate([block0[1], near[1]], axis=0)
     far0 = exchange(after(jnp.concatenate([cot0, token0[2]], axis=1), payload1), 0)
     token1 = split(block2[0], 0)
-    far1 = exchange(after(jnp.concatenate([block2[1], token1[2]], axis=1), payload2), 0)
 
     mine0 = middle(total0, after(arrived0, payload1))
     other0 = send(mine0, core=1)
     pair0 = pair_rows(mine0, other0)
+    far1 = exchange(jnp.concatenate([block2[1], token1[2], pair0[3]], axis=1), 0)
 
-    mine1 = middle(total1, arrived1)
+    mine1 = middle(total1, after(arrived1, far0))
     other1 = send(mine1, core=1)
-    pair1 = pair_rows(after(mine1, far0), other1)
-    mine2 = middle(total2, after(arrived2, other1, pair1[3]))
-    other2 = send(mine2, core=1)
-    pair2 = pair_rows(after(mine2, pair0[3], far1), other2)
+    pair1 = pair_rows(mine1, other1)
+    got1 = exchange(pair1[3], 0)
+    result1 = back(after(mine1, pair1[3]), other1, weights).astype(BF)
+    mine2 = middle(total2, after(arrived2, pair1[3]))
+    other2 = send(after(mine2, result1), core=1)
+    pair2 = pair_rows(after(mine2, far1, far0), other2)
+    got2 = exchange(pair2[3], 0)
 
     cot_pair = jnp.concatenate([cot0, block2[1], far0[:, :1536], far1[:, :1536]], axis=0)
     token_own = jnp.concatenate([token0[0], token1[0], far0[:, 1536:1920], far1[:, 1536:1920]], axis=0)
-    token_second = jnp.concatenate([token0[1], token1[1], far0[:, 1920:], far1[:, 1920:]], axis=0)
+    token_second = jnp.concatenate([token0[1], token1[1], far0[:, 1920:], far1[:, 1920:2304]], axis=0)
     cot_pair, token_own, token_second = lax.optimization_barrier((cot_pair, token_own, token_second))
 
     pairs = (pair0, pair1, pair2)
+    gots = (far1[:, 2304:], got1, got2)
 
     def joined(i, cols):
-        return jnp.concatenate([p[i] for p in pairs] + [p[3][:, cols] for p in pairs], axis=0)
+        return jnp.concatenate([p[i] for p in pairs] + [p[:, cols] for p in gots], axis=0)
 
     act_own = joined(0, slice(0, 384))
     act_second = joined(1, slice(384, 768))
     grad_pair = joined(2, slice(768, 2304))
     act_own, act_second, grad_pair = lax.optimization_barrier((act_own, act_second, grad_pair))
     out_sent = dot(act_second, cot_pair, (0, 0)).astype(BF)
-    in_sent = dot(token_second, grad_pair, (0, 0)).astype(BF)
     out_kept, in_kept = lax.optimization_barrier(
         (dot(act_own, cot_pair, (0, 0)), dot(token_own, grad_pair, (0, 0)))
     )
+    in_sent = dot(after(token_second, out_kept, in_kept), grad_pair, (0, 0)).astype(BF)
     grad_w_out = (out_kept + exchange(out_sent, 1).astype(F32)).astype(BF)
     grad_w_in = (in_kept + exchange(in_sent, 1).astype(F32)).astype(BF)
 
-    result0 = back(after(mine0, mine2), other0, weights)
-    result1 = back(mine1, other1, weights).astype(BF)
-    result2 = back(mine2, other2, weights).astype(BF)
-    got1 = send(result1[:, :96], x=1)
-    got3 = send(result1[:, 96:], x=3)
-    got2 = send(result2, x=2)
-    total = result0 + got1.astype(F32) + got3.astype(F32) + got2.astype(F32)
+    result0 = back(after(mine0, pair2[3]), other0, weights)
+    result2 = back(after(mine2, pair2[3]), other2, weights).astype(BF)
+    total = result0
+    for part in (send(result1[:, :96], x=1), send(result1[:, 96:], x=3), send(result2, x=2)):
+        total = total + part.astype(F32)
     total = after(total, out_sent, in_sent)
+    arrived = [send(total[:, 24 * k : 24 * k + 24].astype(BF), lo=k) for k in (1, 2, 3)]
+
     sums = total[:, :24]
-    for k in (1, 2, 3):
-        sums = sums + send(total[:, 24 * k : 24 * k + 24].astype(BF), lo=k).astype(F32)
+    for part in arrived:
+        sums = sums + after(part, grad_w_out, grad_w_in).astype(F32)
     layer_out = sums[0].astype(BF)
     grad_tokens = sums[1].astype(BF)
-
     return (layer_out, grad_tokens, grad_w_in, grad_w_out)
 
 

time: 154 us -> 154 us (level); the launches traced: 154 us -> 151 us
  waiting for transfers between devices: 68.6 us -> 57.9 us
  starting transfers between devices: 45 us -> 52.6 us
    ppermute x7 -> x6, waiting for transfers between devices: 35.3 us -> 10.9 us  [exchange(): return lax.ppermute(array, AXES, pairs)]
    ppermute x21 -> x22, waiting for transfers between devices: 33.3 us -> 47 us  [send(): return lax.ppermute(array, AXES, pairs)]
    ppermute x21 -> x22, starting transfers between devices: 34.3 us -> 43.6 us  [send(): return lax.ppermute(array, AXES, pairs)]
    ppermute x7 -> x6, starting transfers between devices: 10.7 us -> 9.06 us  [exchange(): return lax.ppermute(array, AXES, pairs)]
  transfers between devices with their start and end apart: 28 -> 28, of which waited for: 15 -> 12; matrix products, arithmetic and copies ran while one was open for 23% -> 24% of each run, Pallas kernels for 0% -> 0%
where the time goes in v2:
time: 154 us; the launch traced here: 151 us
  waiting for transfers between devices  57.9 us (38%)
  starting transfers between devices  52.6 us (34%)
  matrix products  21.4 us (14%)
  other arithmetic  9.03 us (6%)
  local copies, waits for them, and re-layouts  8.88 us (6%)
    ppermute x22, waiting for transfers between devices, send(): return lax.ppermute(array, AXES, pairs)  47 us
    ppermute x22, starting transfers between devices, send(): return lax.ppermute(array, AXES, pairs)  43.6 us
    dot_general x28, matrix products, dot(): lax.dot_general(left, right, ((dims[:1], dims[1:]), ((), ())), preferred_...  21.4 us
    ppermute x6, waiting for transfers between devices, exchange(): return lax.ppermute(array, AXES, pairs)  10.9 us
    ppermute x6, starting transfers between devices, exchange(): return lax.ppermute(array, AXES, pairs)  9.06 us
    dynamic_slice x1, local copies, waits for them, and re-layouts, local(): lax.dynamic_slice_in_dim(w_in, (1 - core) * 768, 768, axis=1)  4.96 us
  transfers between devices with their start and end apart: 28, of which 12 were waited for; matrix products, arithmetic and copies ran while one was open for 24% of the time, Pallas kernels for 0%

profile of v2, /device:TPU:32, one launch (start us, length us, event | category | flops | bytes accessed | tf_op | source)
XLA Modules:
  0.0 151.3 jit_solution(14197872088907607506)
XLA Ops:
  0.6 1.7 %pad_maximum_fusion.15 = bf16[2,24,1536]{2,1,0:T(8,128)(2,1)} fusion(bf16[1,24,1536]{2,1,0:T(8,128)(2,1)} %bitcast.209, bf16[1,24,1536]{2,1,0:T(8,128)(2,1)} %bitcast.211), kind=kLoop, calls=%fused_computation.204 | loop fusion | flops 73728 | bytes 294912 | tf_op jit(solution)/shard_map/stack | solution.py:94
  2.3 1.9 %collective-permute-start.2 = (bf16[2,24,1536]{2,1,0:T(8,128)(2,1)}, bf16[2,24,1536]{2,1,0:T(8,128)(2,1)S(1)}, u32[]{:S(2)}, u32[]{:S(2)}) collective-permute-start(bf16[2,24,1536]{2,1,0:T(8,128)(2,1)} %pad_maximum_fusion.15), channel_id=1, source_target_pairs={{0,16},{1,17},{2,18},{3,19},{4,20},{5,21},{6,22},{7,23},{8,24},{9,... | collective-permute-start | bytes 442376 | tf_op jit(solution)/shard_map/ppermute | solution.py:35
  4.2 2.3 %collective-permute-start.1 = (bf16[2,24,1536]{2,1,0:T(8,128)(2,1)}, bf16[2,24,1536]{2,1,0:T(8,128)(2,1)S(1)}, u32[]{:S(2)}, u32[]{:S(2)}) collective-permute-start(bf16[2,24,1536]{2,1,0:T(8,128)(2,1)} %pad_maximum_fusion.15), channel_id=1, source_target_pairs={{0,32},{1,33},{2,34},{3,35},{4,36},{5,37},{6,38},{7,39},{8,40},{9,... | collective-permute-start | bytes 442376 | tf_op jit(solution)/shard_map/ppermute | solution.py:35
  6.5 1.1 collective-permute-start
  7.6 5.0 %constant_dynamic-slice_fusion.2 = (bf16[1536,768]{1,0:T(8,128)(2,1)}, bf16[1536,768]{1,0:T(8,128)(2,1)}) fusion(bf16[1536,1536]{1,0:T(8,128)(2,1)} %param.5, s32[]{:T(128)S(6)} %select_n.141, s32[]{:T(128)S(6)} %select_n.140), kind=kLoop, calls=%fused_computation.254 | loop fusion | bytes 9437192 | tf_op jit(solution)/shard_map/dynamic_slice | solution.py:86
  12.6 1.7 %constant_dynamic-slice_fusion = (bf16[768,1536]{1,0:T(8,128)(2,1)}, bf16[768,1536]{1,0:T(8,128)(2,1)S(1)}) fusion(bf16[1536,1536]{1,0:T(8,128)(2,1)S(1)} %bitcast.208, s32[]{:T(128)S(6)} %select_n.141, s32[]{:T(128)S(6)} %select_n.140), kind=kLoop, calls=%fused_computation.252 | loop fusion | bytes 9437192 | tf_op jit(solution)/shard_map/dynamic_slice | solution.py:88
  15.1 2.0 %collective-permute-done.1 = bf16[2,24,1536]{2,1,0:T(8,128)(2,1)S(1)} collective-permute-done((bf16[2,24,1536]{2,1,0:T(8,128)(2,1)}, bf16[2,24,1536]{2,1,0:T(8,128)(2,1)S(1)}, u32[]{:S(2)}, u32[]{:S(2)}) %collective-permute-start.1) | collective-permute-done | bytes 147488 | tf_op jit(solution)/shard_map/ppermute | solution.py:35
  17.1 2.0 %collective-permute-done = bf16[2,24,1536]{2,1,0:T(8,128)(2,1)S(1)} collective-permute-done((bf16[2,24,1536]{2,1,0:T(8,128)(2,1)}, bf16[2,24,1536]{2,1,0:T(8,128)(2,1)S(1)}, u32[]{:S(2)}, u32[]{:S(2)}) %collective-permute-start) | collective-permute-done | bytes 147488 | tf_op jit(solution)/shard_map/ppermute | solution.py:35
  19.2 1.6 %collective-permute-start.6 = (bf16[2,96,1536]{2,1,0:T(8,128)(2,1)S(1)}, bf16[2,96,1536]{2,1,0:T(8,128)(2,1)S(1)}, u32[]{:S(2)}, u32[]{:S(2)}) collective-permute-start(bf16[2,96,1536]{2,1,0:T(8,128)(2,1)S(1)} %pad_maximum_fusion.3), channel_id=1, source_target_pairs={{0,4},{1,5},{2,6},{3,7},{4,8},{5,9},{6,10},{7,11},{8,12},{9,13},{1... | collective-permute-start | bytes 1769480 | tf_op jit(solution)/shard_map/ppermute | solution.py:35
  20.8 1.7 %collective-permute-start.5 = (bf16[2,96,1536]{2,1,0:T(8,128)(2,1)S(1)}, bf16[2,96,1536]{2,1,0:T(8,128)(2,1)S(1)}, u32[]{:S(2)}, u32[]{:S(2)}) collective-permute-start(bf16[2,96,1536]{2,1,0:T(8,128)(2,1)S(1)} %pad_maximum_fusion.3), channel_id=1, source_target_pairs={{0,12},{1,13},{2,14},{3,15},{4,0},{5,1},{6,2},{7,3},{8,4},{9,5},{1... | collective-permute-start | bytes 1769480 | tf_op jit(solution)/shard_map/ppermute | solution.py:35
  23.1 0.8 fusion.15
  25.3 0.8 convolution_bitcast_fusion.4
  26.2 6.1 %collective-permute-start.4 = (bf16[2,96,768]{2,1,0:T(8,128)(2,1)S(1)}, bf16[2,96,768]{2,1,0:T(8,128)(2,1)S(1)}, u32[]{:S(2)}, u32[]{:S(2)}) collective-permute-start(bf16[2,96,768]{2,1,0:T(8,128)(2,1)S(1)} %fusion.36), channel_id=1, source_target_pairs={{0,128},{1,129},{2,130},{3,131},{4,132},{5,133},{6,134},{7,135},{8... | collective-permute-start | bytes 884744 | tf_op jit(solution)/shard_map/ppermute | solution.py:35
  32.3 3.5 %collective-permute-done.5 = bf16[2,96,1536]{2,1,0:T(8,128)(2,1)S(1)} collective-permute-done((bf16[2,96,1536]{2,1,0:T(8,128)(2,1)S(1)}, bf16[2,96,1536]{2,1,0:T(8,128)(2,1)S(1)}, u32[]{:S(2)}, u32[]{:S(2)}) %collective-permute-start.5) | collective-permute-done | bytes 589856 | tf_op jit(solution)/shard_map/ppermute | solution.py:35
  36.6 0.9 fusion.13
  37.5 1.6 %collective-permute-start.9 = (bf16[96,1536]{1,0:T(8,128)(2,1)S(1)}, bf16[96,1536]{1,0:T(8,128)(2,1)S(1)}, u32[]{:S(2)}, u32[]{:S(2)}) collective-permute-start(bf16[96,1536]{1,0:T(8,128)(2,1)S(1)} %slice_bitcast_fusion.4), channel_id=1, source_target_pairs={{0,4},{1,5},{2,6},{3,7},{4,8},{5,9},{6,10},{7,11},{8,12},{9,13},{1... | collective-permute-start | bytes 884744 | tf_op jit(solution)/shard_map/ppermute | solution.py:35
  39.1 1.8 %collective-permute-start.8 = (bf16[96,1536]{1,0:T(8,128)(2,1)S(1)}, bf16[96,1536]{1,0:T(8,128)(2,1)S(1)}, u32[]{:S(2)}, u32[]{:S(2)}) collective-permute-start(bf16[96,1536]{1,0:T(8,128)(2,1)S(1)} %slice_bitcast_fusion.5), channel_id=1, source_target_pairs={{0,12},{1,13},{2,14},{3,15},{4,0},{5,1},{6,2},{7,3},{8,4},{9,5},{1... | collective-permute-start | bytes 884744 | tf_op jit(solution)/shard_map/ppermute | solution.py:35
  42.2 0.9 convolution_bitcast_fusion
  43.2 3.7 %collective-permute-done.9 = bf16[96,1536]{1,0:T(8,128)(2,1)S(1)} collective-permute-done((bf16[96,1536]{1,0:T(8,128)(2,1)S(1)}, bf16[96,1536]{1,0:T(8,128)(2,1)S(1)}, u32[]{:S(2)}, u32[]{:S(2)}) %collective-permute-start.9) | collective-permute-done | bytes 294944 | tf_op jit(solution)/shard_map/ppermute | solution.py:35
  47.6 0.8 fusion.17
  49.0 5.7 %collective-permute-start.12 = (bf16[2,192,768]{2,1,0:T(8,128)(2,1)S(1)}, bf16[2,192,768]{2,1,0:T(8,128)(2,1)S(1)}, u32[]{:S(2)}, u32[]{:S(2)}) collective-permute-start(bf16[2,192,768]{2,1,0:T(8,128)(2,1)S(1)} %fusion.18), channel_id=1, source_target_pairs={{0,128},{1,129},{2,130},{3,131},{4,132},{5,133},{6,134},{7,135},{8... | collective-permute-start | bytes 1769480 | tf_op jit(solution)/shard_map/ppermute | solution.py:35
  54.7 0.8 convolution_bitcast_fusion.2
  56.8 1.7 %collective-permute-start.13 = (bf16[288,2304]{1,0:T(8,128)(2,1)S(1)}, bf16[288,2304]{1,0:T(8,128)(2,1)S(1)}, u32[]{:S(2)}, u32[]{:S(2)}) collective-permute-start(bf16[288,2304]{1,0:T(8,128)(2,1)S(1)} %pad_maximum_fusion.1), channel_id=1, source_target_pairs={{0,1},{1,0},{2,3},{3,2},{4,5},{5,4},{6,7},{7,6},{8,9},{9,8},{10,11... | collective-permute-start | bytes 3981320 | tf_op jit(solution)/shard_map/ppermute | solution.py:45
  59.4 1.2 collective-permute-start.16
  60.7 23.1 %collective-permute-done.12 = bf16[2,192,768]{2,1,0:T(8,128)(2,1)S(1)} collective-permute-done((bf16[2,192,768]{2,1,0:T(8,128)(2,1)S(1)}, bf16[2,192,768]{2,1,0:T(8,128)(2,1)S(1)}, u32[]{:S(2)}, u32[]{:S(2)}) %collective-permute-start.12) | collective-permute-done | bytes 589856 | tf_op jit(solution)/shard_map/ppermute | solution.py:35
  84.9 1.9 %collective-permute-done.14 = bf16[2,192,768]{2,1,0:T(8,128)(2,1)S(1)} collective-permute-done((bf16[2,192,768]{2,1,0:T(8,128)(2,1)S(1)}, bf16[2,192,768]{2,1,0:T(8,128)(2,1)S(1)}, u32[]{:S(2)}, u32[]{:S(2)}) %collective-permute-start.14) | collective-permute-done | bytes 589856 | tf_op jit(solution)/shard_map/ppermute | solution.py:35
  87.7 1.7 %collective-permute-start.21 = (bf16[192,2304]{1,0:T(8,128)(2,1)S(1)}, bf16[192,2304]{1,0:T(8,128)(2,1)S(1)}, u32[]{:S(2)}, u32[]{:S(2)}) collective-permute-start(bf16[192,2304]{1,0:T(8,128)(2,1)S(1)} %pad_maximum_fusion.2), channel_id=1, source_target_pairs={{0,1},{1,0},{2,3},{3,2},{4,5},{5,4},{6,7},{7,6},{8,9},{9,8},{10,11... | collective-permute-start | bytes 2654216 | tf_op jit(solution)/shard_map/ppermute | solution.py:45
  90.4 0.9 fusion.58
  92.0 10.9 %collective-permute-start.17 = (bf16[2,96,768]{2,1,0:T(8,128)(2,1)S(1)}, bf16[2,96,768]{2,1,0:T(8,128)(2,1)S(1)}, u32[]{:S(2)}, u32[]{:S(2)}) collective-permute-start(bf16[2,96,768]{2,1,0:T(8,128)(2,1)S(1)} %pad_maximum_fusion.14), channel_id=1, source_target_pairs={{0,64},{1,65},{2,66},{3,67},{4,68},{5,69},{6,70},{7,71},{8,72},{9,... | collective-permute-start | bytes 884744 | tf_op jit(solution)/shard_map/ppermute | solution.py:35
  102.9 0.9 fusion.4
  104.9 2.9 %collective-permute-start.19 = (bf16[2,96,1536]{2,1,0:T(8,128)(2,1)S(1)}, bf16[2,96,1536]{2,1,0:T(8,128)(2,1)S(1)}, u32[]{:S(2)}, u32[]{:S(2)}) collective-permute-start(bf16[2,96,1536]{2,1,0:T(8,128)(2,1)S(1)} %get-tuple-element.72), channel_id=1, source_target_pairs={{0,12},{1,13},{2,14},{3,15},{4,0},{5,1},{6,2},{7,3},{8,4},{9,5},{1... | collective-permute-start | bytes 1769480 | tf_op jit(solution)/shard_map/ppermute | solution.py:35
  108.2 1.1 collective-permute-start.22
  109.3 0.8 fusion.80
  110.7 0.8 fusion.84
  111.5 0.8 fusion.8
  113.9 0.8 fusion.3
  116.6 1.1 convolution_convert_fusion.1
  117.8 1.1 fusion.113
  118.9 2.5 %collective-permute-start.24 = (bf16[384,1536]{1,0:T(8,128)(2,1)S(1)}, bf16[384,1536]{1,0:T(8,128)(2,1)S(1)}, u32[]{:S(2)}, u32[]{:S(2)}) collective-permute-start(bf16[384,1536]{1,0:T(8,128)(2,1)S(1)} %convolution_convert_fusion.1), channel_id=1, source_target_pairs={{0,3},{1,2},{2,1},{3,0},{4,7},{5,6},{6,5},{7,4},{8,11},{9,10},{10,... | collective-permute-start | bytes 3538952 | tf_op jit(solution)/shard_map/ppermute | solution.py:45
  121.4 1.1 fusion.114
  122.5 1.1 convolution_convert_fusion
  123.6 0.9 collective-permute-start.25
  124.5 8.5 %collective-permute-done.19 = bf16[2,96,1536]{2,1,0:T(8,128)(2,1)S(1)} collective-permute-done((bf16[2,96,1536]{2,1,0:T(8,128)(2,1)S(1)}, bf16[2,96,1536]{2,1,0:T(8,128)(2,1)S(1)}, u32[]{:S(2)}, u32[]{:S(2)}) %collective-permute-start.19) | collective-permute-done | bytes 589856 | tf_op jit(solution)/shard_map/ppermute | solution.py:35
  134.1 1.7 %collective-permute-start.23 = (bf16[2,24,1536]{2,1,0:T(8,128)(2,1)S(1)}, bf16[2,24,1536]{2,1,0:T(8,128)(2,1)S(1)}, u32[]{:S(2)}, u32[]{:S(2)}) collective-permute-start(bf16[2,24,1536]{2,1,0:T(8,128)(2,1)S(1)} %get-tuple-element.89), channel_id=1, source_target_pairs={{0,16},{1,17},{2,18},{3,19},{4,20},{5,21},{6,22},{7,23},{8,24},{9,... | collective-permute-start | bytes 442376 | tf_op jit(solution)/shard_map/ppermute | solution.py:35
  136.2 1.1 collective-permute-start.26
  137.4 1.4 add_convert_fusion.1
  138.8 10.2 %collective-permute-done.25 = bf16[384,1536]{1,0:T(8,128)(2,1)S(1)} collective-permute-done((bf16[384,1536]{1,0:T(8,128)(2,1)S(1)}, bf16[384,1536]{1,0:T(8,128)(2,1)S(1)}, u32[]{:S(2)}, u32[]{:S(2)}) %collective-permute-start.25) | collective-permute-done | bytes 1179680 | tf_op jit(solution)/shard_map/ppermute | solution.py:45
  149.0 1.4 add_convert_fusion
  (124 shorter events, 19.5 us)
Async XLA Ops:
  0.6 11.9 %slice-start = ((s8[4718592]{0:T(1024)(128)(4,1)}), s8[524288]{0:T(1024)(128)(4,1)S(1)}, s32[]{:S(2)}) async-start(s8[4718592]{0:T(1024)(128)(4,1)} %bitcast.207), calls=%async_computation | async-start | bytes 1048576
  2.3 12.8 %collective-permute-start.2 = (bf16[2,24,1536]{2,1,0:T(8,128)(2,1)}, bf16[2,24,1536]{2,1,0:T(8,128)(2,1)S(1)}, u32[]{:S(2)}, u32[]{:S(2)}) collective-permute-start(bf16[2,24,1536]{2,1,0:T(8,128)(2,1)} %pad_maximum_fusion.15), channel_id=1, source_target_pairs={{0,16},{1,17},{2,18},{3,19},{4,20},{5,21},{6,22},{7,23},{8,24},{9,... | collective-permute-start | bytes 442376 | tf_op jit(solution)/shard_map/ppermute | solution.py:35
  4.2 12.9 %collective-permute-start.1 = (bf16[2,24,1536]{2,1,0:T(8,128)(2,1)}, bf16[2,24,1536]{2,1,0:T(8,128)(2,1)S(1)}, u32[]{:S(2)}, u32[]{:S(2)}) collective-permute-start(bf16[2,24,1536]{2,1,0:T(8,128)(2,1)} %pad_maximum_fusion.15), channel_id=1, source_target_pairs={{0,32},{1,33},{2,34},{3,35},{4,36},{5,37},{6,38},{7,39},{8,40},{9,... | collective-permute-start | bytes 442376 | tf_op jit(solution)/shard_map/ppermute | solution.py:35
  6.5 12.6 %collective-permute-start = (bf16[2,24,1536]{2,1,0:T(8,128)(2,1)}, bf16[2,24,1536]{2,1,0:T(8,128)(2,1)S(1)}, u32[]{:S(2)}, u32[]{:S(2)}) collective-permute-start(bf16[2,24,1536]{2,1,0:T(8,128)(2,1)} %pad_maximum_fusion.15), channel_id=1, source_target_pairs={{0,48},{1,49},{2,50},{3,51},{4,52},{5,53},{6,54},{7,55},{8,56},{9,... | collective-permute-start | bytes 442376 | tf_op jit(solution)/shard_map/ppermute | solution.py:35
  7.6 5.0 %slice-start.1 = ((s8[4718592]{0:T(1024)(128)(4,1)}), s8[4194304]{0:T(1024)(128)(4,1)S(1)}, s32[]{:S(2)}) async-start(s8[4718592]{0:T(1024)(128)(4,1)} %bitcast.207), calls=%async_computation.1 | async-start | bytes 8388608
  12.6 6.5 %copy-start.3 = (bf16[24,1536]{1,0:T(8,128)(2,1)S(1)}, bf16[24,1536]{1,0:T(8,128)(2,1)}, u32[]{:S(2)}) copy-start(bf16[24,1536]{1,0:T(8,128)(2,1)} %param.7) | copy-start | bytes 221188
  12.6 6.5 %copy-start.4 = (bf16[24,1536]{1,0:T(8,128)(2,1)S(1)}, bf16[24,1536]{1,0:T(8,128)(2,1)}, u32[]{:S(2)}) copy-start(bf16[24,1536]{1,0:T(8,128)(2,1)} %param.4) | copy-start | bytes 221188
  14.3 8.3 %copy-start.1 = (bf16[1536,768]{1,0:T(8,128)(2,1)S(1)}, bf16[1536,768]{1,0:T(8,128)(2,1)}, u32[]{:S(2)}) copy-start(bf16[1536,768]{1,0:T(8,128)(2,1)} %get-tuple-element.33) | copy-start | bytes 7077892
  19.2 3.9 %copy-start = (bf16[768,1536]{1,0:T(8,128)(2,1)S(1)}, bf16[768,1536]{1,0:T(8,128)(2,1)}, u32[]{:S(2)}) copy-start(bf16[768,1536]{1,0:T(8,128)(2,1)} %get-tuple-element.34) | copy-start | bytes 7077892
  19.2 16.6 %collective-permute-start.6 = (bf16[2,96,1536]{2,1,0:T(8,128)(2,1)S(1)}, bf16[2,96,1536]{2,1,0:T(8,128)(2,1)S(1)}, u32[]{:S(2)}, u32[]{:S(2)}) collective-permute-start(bf16[2,96,1536]{2,1,0:T(8,128)(2,1)S(1)} %pad_maximum_fusion.3), channel_id=1, source_target_pairs={{0,4},{1,5},{2,6},{3,7},{4,8},{5,9},{6,10},{7,11},{8,12},{9,13},{1... | collective-permute-start | bytes 1769480 | tf_op jit(solution)/shard_map/ppermute | solution.py:35
  20.8 15.0 %collective-permute-start.5 = (bf16[2,96,1536]{2,1,0:T(8,128)(2,1)S(1)}, bf16[2,96,1536]{2,1,0:T(8,128)(2,1)S(1)}, u32[]{:S(2)}, u32[]{:S(2)}) collective-permute-start(bf16[2,96,1536]{2,1,0:T(8,128)(2,1)S(1)} %pad_maximum_fusion.3), channel_id=1, source_target_pairs={{0,12},{1,13},{2,14},{3,15},{4,0},{5,1},{6,2},{7,3},{8,4},{9,5},{1... | collective-permute-start | bytes 1769480 | tf_op jit(solution)/shard_map/ppermute | solution.py:35
  23.1 1.7 %copy-start.2 = (bf16[1536,768]{1,0:T(8,128)(2,1)S(1)}, bf16[1536,768]{1,0:T(8,128)(2,1)}, u32[]{:S(2)}) copy-start(bf16[1536,768]{1,0:T(8,128)(2,1)} %get-tuple-element.31) | copy-start | bytes 7077892
  24.0 2.1 %collective-permute-start.3 = (bf16[2,96,768]{2,1,0:T(8,128)(2,1)S(1)}, bf16[2,96,768]{2,1,0:T(8,128)(2,1)S(1)}, u32[]{:S(2)}, u32[]{:S(2)}) collective-permute-start(bf16[2,96,768]{2,1,0:T(8,128)(2,1)S(1)} %pad_maximum_fusion.11), channel_id=1, source_target_pairs={{0,64},{1,65},{2,66},{3,67},{4,68},{5,69},{6,70},{7,71},{8,72},{9,... | collective-permute-start | bytes 884744 | tf_op jit(solution)/shard_map/ppermute | solution.py:35
  26.2 29.3 %collective-permute-start.4 = (bf16[2,96,768]{2,1,0:T(8,128)(2,1)S(1)}, bf16[2,96,768]{2,1,0:T(8,128)(2,1)S(1)}, u32[]{:S(2)}, u32[]{:S(2)}) collective-permute-start(bf16[2,96,768]{2,1,0:T(8,128)(2,1)S(1)} %fusion.36), channel_id=1, source_target_pairs={{0,128},{1,129},{2,130},{3,131},{4,132},{5,133},{6,134},{7,135},{8... | collective-permute-start | bytes 884744 | tf_op jit(solution)/shard_map/ppermute | solution.py:35
  37.5 9.3 %collective-permute-start.9 = (bf16[96,1536]{1,0:T(8,128)(2,1)S(1)}, bf16[96,1536]{1,0:T(8,128)(2,1)S(1)}, u32[]{:S(2)}, u32[]{:S(2)}) collective-permute-start(bf16[96,1536]{1,0:T(8,128)(2,1)S(1)} %slice_bitcast_fusion.4), channel_id=1, source_target_pairs={{0,4},{1,5},{2,6},{3,7},{4,8},{5,9},{6,10},{7,11},{8,12},{9,13},{1... | collective-permute-start | bytes 884744 | tf_op jit(solution)/shard_map/ppermute | solution.py:35
  39.1 7.7 %collective-permute-start.8 = (bf16[96,1536]{1,0:T(8,128)(2,1)S(1)}, bf16[96,1536]{1,0:T(8,128)(2,1)S(1)}, u32[]{:S(2)}, u32[]{:S(2)}) collective-permute-start(bf16[96,1536]{1,0:T(8,128)(2,1)S(1)} %slice_bitcast_fusion.5), channel_id=1, source_target_pairs={{0,12},{1,13},{2,14},{3,15},{4,0},{5,1},{6,2},{7,3},{8,4},{9,5},{1... | collective-permute-start | bytes 884744 | tf_op jit(solution)/shard_map/ppermute | solution.py:35
  41.0 5.9 %collective-permute-start.7 = (bf16[2,192,768]{2,1,0:T(8,128)(2,1)S(1)}, bf16[2,192,768]{2,1,0:T(8,128)(2,1)S(1)}, u32[]{:S(2)}, u32[]{:S(2)}) collective-permute-start(bf16[2,192,768]{2,1,0:T(8,128)(2,1)S(1)} %pad_maximum_fusion.4), channel_id=1, source_target_pairs={{0,64},{1,65},{2,66},{3,67},{4,68},{5,69},{6,70},{7,71},{8,72},{9,... | collective-permute-start | bytes 1769480 | tf_op jit(solution)/shard_map/ppermute | solution.py:35
  49.0 34.9 %collective-permute-start.12 = (bf16[2,192,768]{2,1,0:T(8,128)(2,1)S(1)}, bf16[2,192,768]{2,1,0:T(8,128)(2,1)S(1)}, u32[]{:S(2)}, u32[]{:S(2)}) collective-permute-start(bf16[2,192,768]{2,1,0:T(8,128)(2,1)S(1)} %fusion.18), channel_id=1, source_target_pairs={{0,128},{1,129},{2,130},{3,131},{4,132},{5,133},{6,134},{7,135},{8... | collective-permute-start | bytes 1769480 | tf_op jit(solution)/shard_map/ppermute | solution.py:35
  56.0 3.0 %collective-permute-start.15 = (bf16[2,96,768]{2,1,0:T(8,128)(2,1)S(1)}, bf16[2,96,768]{2,1,0:T(8,128)(2,1)S(1)}, u32[]{:S(2)}, u32[]{:S(2)}) collective-permute-start(bf16[2,96,768]{2,1,0:T(8,128)(2,1)S(1)} %pad_maximum_fusion.12), channel_id=1, source_target_pairs={{0,64},{1,65},{2,66},{3,67},{4,68},{5,69},{6,70},{7,71},{8,72},{9,... | collective-permute-start | bytes 884744 | tf_op jit(solution)/shard_map/ppermute | solution.py:35
  56.1 2.4 %collective-permute-start.10 = (bf16[2,96,768]{2,1,0:T(8,128)(2,1)S(1)}, bf16[2,96,768]{2,1,0:T(8,128)(2,1)S(1)}, u32[]{:S(2)}, u32[]{:S(2)}) collective-permute-start(bf16[2,96,768]{2,1,0:T(8,128)(2,1)S(1)} %pad_maximum_fusion.13), channel_id=1, source_target_pairs={{0,64},{1,65},{2,66},{3,67},{4,68},{5,69},{6,70},{7,71},{8,72},{9,... | collective-permute-start | bytes 884744 | tf_op jit(solution)/shard_map/ppermute | solution.py:35
  56.8 27.0 %collective-permute-start.13 = (bf16[288,2304]{1,0:T(8,128)(2,1)S(1)}, bf16[288,2304]{1,0:T(8,128)(2,1)S(1)}, u32[]{:S(2)}, u32[]{:S(2)}) collective-permute-start(bf16[288,2304]{1,0:T(8,128)(2,1)S(1)} %pad_maximum_fusion.1), channel_id=1, source_target_pairs={{0,1},{1,0},{2,3},{3,2},{4,5},{5,4},{6,7},{7,6},{8,9},{9,8},{10,11... | collective-permute-start | bytes 3981320 | tf_op jit(solution)/shard_map/ppermute | solution.py:45
  58.6 31.5 %collective-permute-start.11 = (bf16[2,96,768]{2,1,0:T(8,128)(2,1)S(1)}, bf16[2,96,768]{2,1,0:T(8,128)(2,1)S(1)}, u32[]{:S(2)}, u32[]{:S(2)}) collective-permute-start(bf16[2,96,768]{2,1,0:T(8,128)(2,1)S(1)} %fusion.35), channel_id=1, source_target_pairs={{0,128},{1,129},{2,130},{3,131},{4,132},{5,133},{6,134},{7,135},{8... | collective-permute-start | bytes 884744 | tf_op jit(solution)/shard_map/ppermute | solution.py:35
  59.4 32.5 %collective-permute-start.16 = (bf16[96,4608]{1,0:T(8,128)(2,1)S(1)}, bf16[96,4608]{1,0:T(8,128)(2,1)S(1)}, u32[]{:S(2)}, u32[]{:S(2)}) collective-permute-start(bf16[96,4608]{1,0:T(8,128)(2,1)S(1)} %get-tuple-element.58), channel_id=1, source_target_pairs={{0,1},{1,0},{2,3},{3,2},{4,5},{5,4},{6,7},{7,6},{8,9},{9,8},{10,11... | collective-permute-start | bytes 2654216 | tf_op jit(solution)/shard_map/ppermute | solution.py:45
  84.7 2.1 %collective-permute-start.14 = (bf16[2,192,768]{2,1,0:T(8,128)(2,1)S(1)}, bf16[2,192,768]{2,1,0:T(8,128)(2,1)S(1)}, u32[]{:S(2)}, u32[]{:S(2)}) collective-permute-start(bf16[2,192,768]{2,1,0:T(8,128)(2,1)S(1)} %pad_maximum_fusion.6), channel_id=1, source_target_pairs={{0,64},{1,65},{2,66},{3,67},{4,68},{5,69},{6,70},{7,71},{8,72},{9,... | collective-permute-start | bytes 1769480 | tf_op jit(solution)/shard_map/ppermute | solution.py:35
  87.7 28.1 %collective-permute-start.21 = (bf16[192,2304]{1,0:T(8,128)(2,1)S(1)}, bf16[192,2304]{1,0:T(8,128)(2,1)S(1)}, u32[]{:S(2)}, u32[]{:S(2)}) collective-permute-start(bf16[192,2304]{1,0:T(8,128)(2,1)S(1)} %pad_maximum_fusion.2), channel_id=1, source_target_pairs={{0,1},{1,0},{2,3},{3,2},{4,5},{5,4},{6,7},{7,6},{8,9},{9,8},{10,11... | collective-permute-start | bytes 2654216 | tf_op jit(solution)/shard_map/ppermute | solution.py:45
  92.0 16.0 %collective-permute-start.17 = (bf16[2,96,768]{2,1,0:T(8,128)(2,1)S(1)}, bf16[2,96,768]{2,1,0:T(8,128)(2,1)S(1)}, u32[]{:S(2)}, u32[]{:S(2)}) collective-permute-start(bf16[2,96,768]{2,1,0:T(8,128)(2,1)S(1)} %pad_maximum_fusion.14), channel_id=1, source_target_pairs={{0,64},{1,65},{2,66},{3,67},{4,68},{5,69},{6,70},{7,71},{8,72},{9,... | collective-permute-start | bytes 884744 | tf_op jit(solution)/shard_map/ppermute | solution.py:35
  104.6 19.9 %collective-permute-start.18 = (bf16[2,96,1536]{2,1,0:T(8,128)(2,1)S(1)}, bf16[2,96,1536]{2,1,0:T(8,128)(2,1)S(1)}, u32[]{:S(2)}, u32[]{:S(2)}) collective-permute-start(bf16[2,96,1536]{2,1,0:T(8,128)(2,1)S(1)} %get-tuple-element.71), channel_id=1, source_target_pairs={{0,4},{1,5},{2,6},{3,7},{4,8},{5,9},{6,10},{7,11},{8,12},{9,13},{1... | collective-permute-start | bytes 1769480 | tf_op jit(solution)/shard_map/ppermute | solution.py:35
  104.9 28.1 %collective-permute-start.19 = (bf16[2,96,1536]{2,1,0:T(8,128)(2,1)S(1)}, bf16[2,96,1536]{2,1,0:T(8,128)(2,1)S(1)}, u32[]{:S(2)}, u32[]{:S(2)}) collective-permute-start(bf16[2,96,1536]{2,1,0:T(8,128)(2,1)S(1)} %get-tuple-element.72), channel_id=1, source_target_pairs={{0,12},{1,13},{2,14},{3,15},{4,0},{5,1},{6,2},{7,3},{8,4},{9,5},{1... | collective-permute-start | bytes 1769480 | tf_op jit(solution)/shard_map/ppermute | solution.py:35
  108.2 8.4 %collective-permute-start.22 = (bf16[96,2304]{1,0:T(8,128)(2,1)S(1)}, bf16[96,2304]{1,0:T(8,128)(2,1)S(1)}, u32[]{:S(2)}, u32[]{:S(2)}) collective-permute-start(bf16[96,2304]{1,0:T(8,128)(2,1)S(1)} %pad_maximum_fusion.10), channel_id=1, source_target_pairs={{0,1},{1,0},{2,3},{3,2},{4,5},{5,4},{6,7},{7,6},{8,9},{9,8},{10,11... | collective-permute-start | bytes 1327112 | tf_op jit(solution)/shard_map/ppermute | solution.py:45
  112.9 20.8 %collective-permute-start.20 = (bf16[2,96,1536]{2,1,0:T(8,128)(2,1)S(1)}, bf16[2,96,1536]{2,1,0:T(8,128)(2,1)S(1)}, u32[]{:S(2)}, u32[]{:S(2)}) collective-permute-start(bf16[2,96,1536]{2,1,0:T(8,128)(2,1)S(1)} %pad_maximum_fusion.7), channel_id=1, source_target_pairs={{0,8},{1,9},{2,10},{3,11},{4,12},{5,13},{6,14},{7,15},{8,0},{9,1},... | collective-permute-start | bytes 1769480 | tf_op jit(solution)/shard_map/ppermute | solution.py:35
  118.9 18.5 %collective-permute-start.24 = (bf16[384,1536]{1,0:T(8,128)(2,1)S(1)}, bf16[384,1536]{1,0:T(8,128)(2,1)S(1)}, u32[]{:S(2)}, u32[]{:S(2)}) collective-permute-start(bf16[384,1536]{1,0:T(8,128)(2,1)S(1)} %convolution_convert_fusion.1), channel_id=1, source_target_pairs={{0,3},{1,2},{2,1},{3,0},{4,7},{5,6},{6,5},{7,4},{8,11},{9,10},{10,... | collective-permute-start | bytes 3538952 | tf_op jit(solution)/shard_map/ppermute | solution.py:45
  123.6 25.4 %collective-permute-start.25 = (bf16[384,1536]{1,0:T(8,128)(2,1)S(1)}, bf16[384,1536]{1,0:T(8,128)(2,1)S(1)}, u32[]{:S(2)}, u32[]{:S(2)}) collective-permute-start(bf16[384,1536]{1,0:T(8,128)(2,1)S(1)} %convolution_convert_fusion), channel_id=1, source_target_pairs={{0,3},{1,2},{2,1},{3,0},{4,7},{5,6},{6,5},{7,4},{8,11},{9,10},{10,... | collective-permute-start | bytes 3538952 | tf_op jit(solution)/shard_map/ppermute | solution.py:45
  134.1 16.2 %collective-permute-start.23 = (bf16[2,24,1536]{2,1,0:T(8,128)(2,1)S(1)}, bf16[2,24,1536]{2,1,0:T(8,128)(2,1)S(1)}, u32[]{:S(2)}, u32[]{:S(2)}) collective-permute-start(bf16[2,24,1536]{2,1,0:T(8,128)(2,1)S(1)} %get-tuple-element.89), channel_id=1, source_target_pairs={{0,16},{1,17},{2,18},{3,19},{4,20},{5,21},{6,22},{7,23},{8,24},{9,... | collective-permute-start | bytes 442376 | tf_op jit(solution)/shard_map/ppermute | solution.py:35
  135.8 14.5 %collective-permute-start.27 = (bf16[2,24,1536]{2,1,0:T(8,128)(2,1)S(1)}, bf16[2,24,1536]{2,1,0:T(8,128)(2,1)S(1)}, u32[]{:S(2)}, u32[]{:S(2)}) collective-permute-start(bf16[2,24,1536]{2,1,0:T(8,128)(2,1)S(1)} %get-tuple-element.90), channel_id=1, source_target_pairs={{0,48},{1,49},{2,50},{3,51},{4,52},{5,53},{6,54},{7,55},{8,56},{9,... | collective-permute-start | bytes 442376 | tf_op jit(solution)/shard_map/ppermute | solution.py:35
  136.2 14.1 %collective-permute-start.26 = (bf16[2,24,1536]{2,1,0:T(8,128)(2,1)S(1)}, bf16[2,24,1536]{2,1,0:T(8,128)(2,1)S(1)}, u32[]{:S(2)}, u32[]{:S(2)}) collective-permute-start(bf16[2,24,1536]{2,1,0:T(8,128)(2,1)S(1)} %get-tuple-element.91), channel_id=1, source_target_pairs={{0,32},{1,33},{2,34},{3,35},{4,36},{5,37},{6,38},{7,39},{8,40},{9,... | collective-permute-start | bytes 442376 | tf_op jit(solution)/shard_map/ppermute | solution.py:35
